TPU v7x, 32 devices: a whole 2x2x4 slice. The times are simulated.
32 devices in a mesh: op: 16 (over z, x, core), sec: 2 (over y).
Axes of the slice: x: 2, y: 2, z: 4, core: 2. Of those that a mesh axis runs over, the one named last changes fastest.
Arguments:
- psi: float32 [640, 2, 640], P('op', 'sec'), may hold values from -6 to 6
- left_env: float32 [16, 2, 640, 640], P('op', 'sec'), may hold values from -0.25 to 0.25
- right_env: float32 [16, 2, 640, 640], P('op', 'sec'), may hold values from -0.0625 to 0.0625
- denominators: float32 [640, 2, 640], P('op', 'sec'), may hold values from 0.5 to 4
- source_sector: int32 [16, 2], replicated, may hold values from 0 to 1
- owner: int32 [2], replicated, may hold values from 0 to 1, each once
- orders: int32 [2], replicated, may hold values from 480 to 640
Outputs:
- new_vector: float32 [640, 2, 640], P('op', 'sec')
- correction: float32 [640, 2, 640], P('op', 'sec')
Inputs may be any that keep to these rules, and one draw needn't show every extreme that they name: `source_sector`: entry (t, s) is the sector from which term t maps into sector s. `owner`: each sector's slot; every slot holds one sector. Only the first orders rows and columns of a sector's block count; the inputs may hold any values beyond them, and the mask removes those entries.
All inputs are finite; a program needn't handle non-finite values.
Results may differ from a plain program's by a relative error of at most 0.0003.
Values sent between devices are 32-bit elements; how exact they have to be, the bound alone decides.
A program may use at most 64 MiB of HBM per device.

v0:
```python
import jax
import jax.numpy as jnp
from jax import lax
from jax.sharding import PartitionSpec as P

EPS = 1e-06
HIGH = lax.Precision.HIGHEST


def slot_sectors(owner):
    slots = jnp.arange(owner.shape[0], dtype=jnp.int32)
    hits = (owner[None, :] == slots[:, None]).astype(jnp.int32)
    return jnp.sum(hits * slots[None, :], axis=1)


def per_device(psi, left_env, right_env, denominators, source_sector, owner, orders):
    rows_here = psi.shape[0]
    sec_here = psi.shape[1]
    width = psi.shape[2]
    term_here = left_env.shape[0]
    op_size = lax.axis_size("op")
    sec_size = lax.axis_size("sec")
    op_pos = lax.axis_index("op")
    sec_pos = lax.axis_index("sec")
    sectors = slot_sectors(owner)
    sectors_here = lax.dynamic_slice_in_dim(sectors, sec_pos * sec_here, sec_here, 0)
    order_here = jnp.take(orders, sectors_here)
    row_ids = op_pos * rows_here + jnp.arange(rows_here, dtype=jnp.int32)
    col_ids = jnp.arange(width, dtype=jnp.int32)
    mask = (
        (row_ids[:, None, None] < order_here[None, :, None])
        & (col_ids[None, None, :] < order_here[None, :, None])
    ).astype(jnp.float32)
    source_all = jnp.take(owner, jnp.take(source_sector, sectors_here, axis=1))
    blocks = term_here * sec_here
    left_flat = left_env.reshape(blocks, width, width)
    right_flat = right_env.reshape(blocks, width, width)
    count = float(rows_here * sec_here * width * op_size * sec_size)

    def apply(vector):
        shard_all = lax.all_gather(vector, "sec", axis=1, tiled=True)
        outgoing = jnp.take(shard_all, source_all.reshape(-1), axis=1).reshape(
            rows_here, op_size, blocks, width
        )
        chosen = lax.all_to_all(outgoing, "op", split_axis=1, concat_axis=0, tiled=True).reshape(
            width, blocks, width
        )
        inner = jnp.einsum("apb,pbc->apc", chosen, right_flat, precision=HIGH)
        product = jnp.einsum("pxa,apc->xpc", left_flat, inner, precision=HIGH)
        whole = product.reshape(width, term_here, sec_here, width).sum(axis=1)
        summed = lax.psum_scatter(whole, "op", scatter_dimension=0, tiled=True)
        return summed * mask

    def partial_sum(first, second):
        return jnp.sum(first * second)

    v_raw = psi * mask
    w_raw = apply(v_raw)
    start_pair = lax.psum(
        jnp.stack([partial_sum(v_raw, v_raw), partial_sum(v_raw, w_raw)]), ("op", "sec")
    )
    norm_raw = start_pair[0] / count
    product_raw = start_pair[1] / count
    scale = 1.0 / jnp.sqrt(norm_raw + EPS)
    v_zero = scale * v_raw
    w_zero = scale * w_raw
    rayleigh = product_raw / (norm_raw + EPS)
    update = (w_zero - rayleigh * v_zero) / denominators
    along = lax.psum(partial_sum(v_zero, update), ("op", "sec")) / count
    update_perp = update - along * v_zero
    tail = lax.psum(partial_sum(update_perp, update_perp), ("op", "sec")) / count
    v_one = update_perp / jnp.sqrt(tail + EPS)
    w_one = apply(v_one)
    sub_pair = lax.psum(
        jnp.stack([partial_sum(v_one, w_one), partial_sum(v_one, w_zero)]), ("op", "sec")
    )
    corner = sub_pair[0] / count
    couple = sub_pair[1] / count
    angle = 0.5 * jnp.arctan2(2.0 * couple, rayleigh - corner)
    sine = jnp.sin(angle)
    cosine = jnp.cos(angle)
    new_vector = sine * v_zero - cosine * v_one
    applied = sine * w_zero - cosine * w_one
    lam = sine * sine * rayleigh + cosine * cosine * corner - 2.0 * sine * cosine * couple
    correction = (applied - lam * new_vector) / denominators
    return (new_vector, correction)


def solution(mesh):
    placed = (
        P("op", "sec", None),
        P("op", "sec", None, None),
        P("op", "sec", None, None),
        P("op", "sec", None),
        P(),
        P(),
        P(),
    )
    return jax.shard_map(
        per_device,
        mesh=mesh,
        in_specs=placed,
        out_specs=(P("op", "sec", None), P("op", "sec", None)),
        check_vma=False,
    )
```

profile of v0, /device:TPU:0, one launch (start us, length us, event | category | flops | bytes accessed | tf_op | source)
XLA Modules:
  0.0 535.5 jit_solution(10081152906613645598)
XLA Ops:
  8.1 1.4 fusion.18
  14.0 1.9 compare_and_fusion
  16.9 6.5 %all_gather.6 = f32[40,2,640]{2,0,1:T(8,128)S(1)} all-gather(f32[40,1,640]{2,0,1:T(8,128)S(1)} %and_select_fusion.2), channel_id=1, replica_groups=mesh['op'=16,'sec'=2] {'sec'}, dimensions={1}, use_global_device_ids=true | all-gather | bytes 307200 | tf_op jit(solution)/shard_map/all_gather | solution.py:41
  24.3 45.8 %all_to_all.30 = f32[40,16,1,640]{3,0,2,1:T(8,128)S(1)} all-to-all(f32[40,16,1,640]{3,0,2,1:T(8,128)S(1)} %select_bitcast_fusion.1), channel_id=1, replica_groups=mesh['op'=16,'sec'=2] {'op'}, dimensions={1} | all-to-all | bytes 3276800 | tf_op jit(solution)/shard_map/all_to_all | solution.py:45
  70.0 4.7 fusion.6
  74.7 9.5 %fusion.8 = f32[640,1,640]{0,2,1:T(8,128)} fusion(f32[640,640]{1,0:T(8,128)S(1)} %fusion.6, f32[1,1,640,640]{3,2,1,0:T(8,128)S(1)} %copy-done.1), kind=kOutput, calls=%fused_computation.12 | convolution fusion | flops 3145728000 | bytes 4915200 | tf_op jit(solution)/shard_map/pxa,apc->xpc/dot_general | solution.py:49
  84.2 4.5 copy.34
  90.6 92.8 %all-reduce.5.cloned.1.call-done = f32[640,1,640]{2,1,0:T(1,128)} async-done(((f32[640,1,640]{2,1,0:T(1,128)}), f32[640,1,640]{2,1,0:T(1,128)}) %all-reduce.5.cloned.1.call-update) | async-done | bytes 1638416
  185.1 1.4 pad_maximum_fusion
  186.5 39.4 %psum.28 = f32[2]{0:T(128)S(1)} all-reduce(f32[2]{0:T(128)S(1)} %pad_maximum_fusion), channel_id=1, replica_groups=mesh['op'=16,'sec'=2] {'op','sec'}, use_global_device_ids=true, to_apply=%region_4.6 | all-reduce | flops 2 | bytes 16 | tf_op jit(solution)/shard_map/psum | solution.py:59
  227.9 2.3 multiply_reduce_fusion.3
  230.2 40.1 %psum.29 = f32[]{:T(128)} all-reduce(f32[]{:T(128)} %get-tuple-element.39), channel_id=1, replica_groups=mesh['op'=16,'sec'=2] {'op','sec'}, use_global_device_ids=true, to_apply=%region_6.8 | all-reduce | flops 1 | bytes 8 | tf_op jit(solution)/shard_map/psum | solution.py:69
  270.9 1.7 multiply_reduce_fusion.2
  272.6 40.5 %psum.30 = f32[]{:T(128)} all-reduce(f32[]{:T(128)} %multiply_reduce_fusion.2), channel_id=1, replica_groups=mesh['op'=16,'sec'=2] {'op','sec'}, use_global_device_ids=true, to_apply=%region_8.10 | all-reduce | flops 1 | bytes 8 | tf_op jit(solution)/shard_map/psum | solution.py:71
  315.5 5.8 %all_gather.7 = f32[40,2,640]{2,0,1:T(8,128)S(1)} all-gather(f32[40,1,640]{2,0,1:T(8,128)S(1)} %broadcast_divide_fusion), channel_id=1, replica_groups=mesh['op'=16,'sec'=2] {'sec'}, dimensions={1}, use_global_device_ids=true | all-gather | bytes 307200 | tf_op jit(solution)/shard_map/all_gather | solution.py:41
  321.3 1.8 gather_fusion.1
  323.1 1.6 select_bitcast_fusion
  324.8 44.4 %all_to_all.31 = f32[40,16,1,640]{3,0,2,1:T(8,128)S(1)} all-to-all(f32[40,16,1,640]{3,0,2,1:T(8,128)S(1)} %select_bitcast_fusion), channel_id=1, replica_groups=mesh['op'=16,'sec'=2] {'op'}, dimensions={1} | all-to-all | bytes 3276800 | tf_op jit(solution)/shard_map/all_to_all | solution.py:45
  369.2 4.7 fusion.4
  373.9 9.3 %fusion.11 = f32[640,1,640]{0,2,1:T(8,128)} fusion(f32[640,640]{1,0:T(8,128)S(1)} %fusion.4, f32[1,1,640,640]{3,2,1,0:T(8,128)S(1)} %copy-done.1), kind=kOutput, calls=%fused_computation.13 | convolution fusion | flops 3145728000 | bytes 4915200 | tf_op jit(solution)/shard_map/pxa,apc->xpc/dot_general | solution.py:49
  383.2 4.5 copy.38
  387.7 94.1 %all-reduce.7.cloned.1.call-done = f32[640,1,640]{2,1,0:T(1,128)} async-done(((f32[640,1,640]{2,1,0:T(1,128)}), f32[640,1,640]{2,1,0:T(1,128)}) %all-reduce.7.cloned.1.call-update) | async-done | bytes 1638416
  483.5 1.4 pad_maximum_fusion.1
  484.9 39.4 %psum.31 = f32[2]{0:T(128)S(1)} all-reduce(f32[2]{0:T(128)S(1)} %pad_maximum_fusion.1), channel_id=1, replica_groups=mesh['op'=16,'sec'=2] {'op','sec'}, use_global_device_ids=true, to_apply=%region_12.14 | all-reduce | flops 2 | bytes 16 | tf_op jit(solution)/shard_map/psum | solution.py:74
  (44 shorter events, 13.7 us)
Async XLA Ops:
  7.2 62.9 %copy-start = (f32[1,1,640,640]{3,2,1,0:T(8,128)S(1)}, f32[1,1,640,640]{3,2,1,0:T(8,128)}, u32[]{:S(2)}) copy-start(f32[1,1,640,640]{3,2,1,0:T(8,128)} %param.11) | copy-start | bytes 4915204
  7.2 176.2 %all-reduce.5.cloned.1.call-start = ((), (), s32[]{:S(2)}) async-start(), calls=%async_computation.2 | async-start | bytes 3276800
  70.0 4.7 copy-start.1
  88.7 0.7 copy-start.9
  88.7 95.6 %copy-start.2 = (f32[40,1,640]{2,1,0:T(1,128)S(1)}, f32[40,1,640]{2,1,0:T(1,128)}, u32[]{:S(2)}) copy-start(f32[40,1,640]{2,1,0:T(1,128)} %param.9) | copy-start | bytes 307204
  88.7 393.1 %all-reduce.7.cloned.1.call-start = ((), (), s32[]{:S(2)}) async-start(), calls=%async_computation.3 | async-start | bytes 3276800
  184.3 129.5 %copy-start.4 = (f32[40,1,640]{2,1,0:T(1,128)}, f32[40,1,640]{2,1,0:T(1,128)S(1)}, u32[]{:S(2)}) copy-start(f32[40,1,640]{2,1,0:T(1,128)S(1)} %constant_dynamic-slice_fusion.1) | copy-start | bytes 307204
  314.8 0.6 copy-start.6
  387.7 95.1 %copy-start.5 = (f32[40,1,640]{2,1,0:T(1,128)S(1)}, f32[40,1,640]{2,1,0:T(1,128)}, u32[]{:S(2)}) copy-start(f32[40,1,640]{2,1,0:T(1,128)} %copy-done.4) | copy-start | bytes 307204
  387.7 95.1 %copy-start.7 = (f32[40,1,640]{2,0,1:T(8,128)S(1)}, f32[40,1,640]{2,0,1:T(8,128)}, u32[]{:S(2)}) copy-start(f32[40,1,640]{2,0,1:T(8,128)} %copy-done.6) | copy-start | bytes 307204
  387.7 139.3 %copy-start.3 = (f32[40,1,640]{2,1,0:T(1,128)S(1)}, f32[40,1,640]{2,1,0:T(1,128)}, u32[]{:S(2)}) copy-start(f32[40,1,640]{2,1,0:T(1,128)} %param.9) | copy-start | bytes 307204
  387.7 139.3 %copy-start.8 = (f32[40,1,640]{2,1,0:T(1,128)S(1)}, f32[40,1,640]{2,1,0:T(1,128)}, u32[]{:S(2)}) copy-start(f32[40,1,640]{2,1,0:T(1,128)} %param.12) | copy-start | bytes 307204
Sparse Core Ops, SparseCore 0:
  88.9 94.4 all-reduce.4
  387.8 93.9 all-reduce.6
where the time goes:
time: 537 us; the launch traced here: 535 us
  blocking collectives  262 us (49%)
  waiting for transfers between devices  187 us (35%)
  matrix products  28.2 us (5%)
  between operations  22.4 us (4%)
  local copies, waits for them, and re-layouts  21.1 us (4%)
  other arithmetic  15 us (3%)
    unnamed x4, waiting for transfers between devices  187 us
    all_to_all x2, blocking collectives, apply(): lax.all_to_all(outgoing, 'op', split_axis=1, concat_axis=0, tiled=True)  90.2 us
    psum x1, blocking collectives, per_device(): lax.psum(partial_sum(update_perp, update_perp), ('op', 'sec')) / count  40.5 us
    psum x1, blocking collectives, per_device(): along = lax.psum(partial_sum(v_zero, update), ('op', 'sec')) / count  40.1 us
    psum x1, blocking collectives, per_device(): lax.psum(jnp.stack([partial_sum(v_raw, v_raw), partial_sum(v_raw, w_raw)]...  39.4 us
    psum x1, blocking collectives, per_device(): lax.psum(jnp.stack([partial_sum(v_one, w_one), partial_sum(v_one, w_zero)...  39.4 us
    dot_general x2, matrix products, apply(): product = jnp.einsum('pxa,apc->xpc', left_flat, inner, precision=HIGH)  18.8 us
    all_gather x2, blocking collectives, apply(): shard_all = lax.all_gather(vector, 'sec', axis=1, tiled=True)  12.3 us
  transfers between devices with their start and end apart: 2, of which 2 were waited for; matrix products, arithmetic and copies ran while one was open for 0% of the time, Pallas kernels for 0%

commit v1 on v0

--- a/solution.py
+++ b/solution.py
@@ -1,10 +1,18 @@
+import functools
+
 import jax
 import jax.numpy as jnp
 from jax import lax
+from jax.experimental import pallas as pl
+from jax.experimental.pallas import tpu as pltpu
 from jax.sharding import PartitionSpec as P
 
 EPS = 1e-06
 HIGH = lax.Precision.HIGHEST
+MESH = pl.DeviceIdType.MESH
+F32 = jnp.float32
+BF16 = jnp.bfloat16
+ROWS = 8
 
 
 def slot_sectors(owner):
@@ -13,7 +21,7 @@
     return jnp.sum(hits * slots[None, :], axis=1)
 
 
-def per_device(psi, left_env, right_env, denominators, source_sector, owner, orders):
+def general(psi, left_env, right_env, denominators, source_sector, owner, orders):
     rows_here = psi.shape[0]
     sec_here = psi.shape[1]
     width = psi.shape[2]
@@ -86,6 +94,419 @@
     return (new_vector, correction)
 
 
+def split(value):
+    high = value.astype(BF16)
+    return high, (value - high.astype(F32)).astype(BF16)
+
+
+def product3(ah, al, bh, bl):
+    dot = functools.partial(jnp.dot, preferred_element_type=F32)
+    return dot(ah, bh) + (dot(ah, bl) + dot(al, bh))
+
+
+def kernel(
+    dims, sec, psi_ref, left_hbm, right_hbm, den_ref, source_ref, owner_ref, orders_ref,
+    new_ref, corr_ref, *scratch
+):
+    far, near, core = dims
+    chunks = psi_ref.shape[0] // ROWS
+    rows = psi_ref.shape[0]
+    width = psi_ref.shape[1]
+    op = far * near * core
+    held = (scratch[:chunks], scratch[chunks : 2 * chunks])
+    (left_f, right_f, left_h, left_l, right_h, right_l, inner, inner_h, inner_l, raw,
+     applied, step, parts, got_core, got_near, got_far, tiles, got_tiles, load_sem,
+     gather_send, gather_recv, sum_send, sum_recv, tile_send, tile_recv) = scratch[2 * chunks :]
+
+    me = lax.axis_index("op")
+    y = lax.axis_index("sec")
+    c = lax.rem(me, core)
+    b = lax.rem(lax.div(me, core), near)
+    a = lax.div(me, core * near)
+    where = {"far": a, "near": b, "core": c, "sec": y}
+    size = {"far": far, "near": near, "core": core, "sec": sec}
+
+    def turned(axis, by):
+        place = dict(where)
+        place[axis] = lax.rem(where[axis] + by + size[axis], size[axis])
+        return place
+
+    def device(place):
+        return ((place["far"] * near + place["near"]) * core + place["core"], place["sec"])
+
+    every = [(axis, d) for axis in ("far", "near", "sec", "core") for d in range(1, size[axis])]
+
+    loads = [
+        pltpu.make_async_copy(right_hbm, right_f, load_sem.at[0]),
+        pltpu.make_async_copy(left_hbm, left_f, load_sem.at[1]),
+    ]
+    for load in loads:
+        load.start()
+
+    barrier = pltpu.get_barrier_semaphore()
+    for axis, d in every:
+        pl.semaphore_signal(
+            barrier, inc=1, device_id=device(turned(axis, d)), device_id_type=MESH
+        )
+
+    sector = jnp.int32(0)
+    for s in range(sec):
+        sector = sector + jnp.where(owner_ref[s] == y, s, 0)
+    order = orders_ref[sector]
+    source = owner_ref[source_ref[me, sector]]
+
+    row_ids = lax.broadcasted_iota(jnp.int32, (rows, width), 0) + me * rows
+    col_ids = lax.broadcasted_iota(jnp.int32, (rows, width), 1)
+    mask = ((row_ids < order) & (col_ids < order)).astype(F32)
+    raw[...] = psi_ref[...] * mask
+    for k in range(chunks):
+        held[0][k][y, a, b, c] = raw[pl.ds(k * ROWS, ROWS), :]
+
+    pl.semaphore_wait(barrier, len(every))
+
+    def area(axes, place):
+        pick = lambda axis: slice(None) if axis in axes else place[axis]
+        return (pick("sec"), pick("far"), pick("near"), pick("core"))
+
+    def sequence(k):
+        return ("far", "near", "sec", "core") if k % 2 == 0 else ("far", "sec", "near", "core")
+
+    slot_of = {pair: n for n, pair in enumerate(every)}
+
+    def gather_copy(turn, k, stage, d, from_place, to_place):
+        axes = sequence(k)
+        block = held[turn][k].at[area(axes[:stage], from_place)]
+        n = slot_of[(axes[stage], d)]
+        return pltpu.make_async_remote_copy(
+            src_ref=block, dst_ref=block,
+            send_sem=gather_send.at[turn, k, n], recv_sem=gather_recv.at[turn, k, n],
+            device_id=device(to_place), device_id_type=MESH,
+        )
+
+    def gather_start(turn, k, stage):
+        axis = sequence(k)[stage]
+        for d in range(1, size[axis]):
+            gather_copy(turn, k, stage, d, where, turned(axis, d)).start()
+
+    def gather_wait(turn, k, stage):
+        axis = sequence(k)[stage]
+        for d in range(1, size[axis]):
+            gather_copy(turn, k, stage, d, turned(axis, -d), turned(axis, d)).wait_recv()
+
+    def gather_end(turn):
+        for k in range(chunks):
+            for stage, axis in enumerate(sequence(k)):
+                for d in range(1, size[axis]):
+                    gather_copy(turn, k, stage, d, where, turned(axis, d)).wait_send()
+
+    def tile_copy(red, stage, d):
+        axis = ("far", "near", "sec", "core")[stage]
+        n = slot_of[(axis, d)]
+        return pltpu.make_async_remote_copy(
+            src_ref=tiles.at[red, stage], dst_ref=got_tiles.at[red, n],
+            send_sem=tile_send.at[red, n], recv_sem=tile_recv.at[red, n],
+            device_id=device(turned(axis, d)), device_id_type=MESH,
+        )
+
+    def tile_start(red, stage, values=None):
+        axis = ("far", "near", "sec", "core")[stage]
+        if values is not None:
+            line = lax.broadcasted_iota(jnp.int32, tiles.shape[2:], 0)
+            tile = jnp.zeros(tiles.shape[2:], F32)
+            for n, value in enumerate(values):
+                tile = jnp.where(line == n, value, tile)
+            tiles[red, stage] = tile
+        for d in range(1, size[axis]):
+            tile_copy(red, stage, d).start()
+
+    def tile_wait(red, stage):
+        axis = ("far", "near", "sec", "core")[stage]
+        total = tiles[red, stage]
+        for d in range(1, size[axis]):
+            tile_copy(red, stage, d).wait_recv()
+            total = total + got_tiles[red, slot_of[(axis, d)]]
+        tiles[red, stage + 1] = total
+
+    def tile_advance(red, stage):
+        tile_wait(red, stage)
+        if stage < 3:
+            tile_start(red, stage + 1)
+
+    count = float(rows * width * op * sec)
+
+    def tile_read(red, n):
+        return tiles[red, 4, pl.ds(n, 1), pl.ds(0, 1)] / count
+
+    def total(value):
+        return jnp.sum(value.reshape(-1, width), keepdims=True)
+
+    def core_copy(turn, k, d):
+        place = turned("core", d)
+        return pltpu.make_async_remote_copy(
+            src_ref=parts.at[turn, k, :, :, place["core"]], dst_ref=got_core.at[turn, k, d - 1],
+            send_sem=sum_send.at[turn, k, slot_of[("core", d)]],
+            recv_sem=sum_recv.at[turn, k, slot_of[("core", d)]],
+            device_id=device(place), device_id_type=MESH,
+        )
+
+    def near_copy(turn, k, d):
+        place = turned("near", d)
+        return pltpu.make_async_remote_copy(
+            src_ref=parts.at[turn, k, :, place["near"], c], dst_ref=got_near.at[turn, k, d - 1],
+            send_sem=sum_send.at[turn, k, slot_of[("near", d)]],
+            recv_sem=sum_recv.at[turn, k, slot_of[("near", d)]],
+            device_id=device(place), device_id_type=MESH,
+        )
+
+    def far_copy(turn, k, d):
+        place = turned("far", d)
+        return pltpu.make_async_remote_copy(
+            src_ref=parts.at[turn, k, place["far"], b, c], dst_ref=got_far.at[turn, k, d - 1],
+            send_sem=sum_send.at[turn, k, slot_of[("far", d)]],
+            recv_sem=sum_recv.at[turn, k, slot_of[("far", d)]],
+            device_id=device(place), device_id_type=MESH,
+        )
+
+    def sum_core(turn, k):
+        for d in range(1, core):
+            core_copy(turn, k, d).wait_recv()
+        mine = parts[turn, k, :, :, c]
+        for d in range(1, core):
+            mine = mine + got_core[turn, k, d - 1]
+        parts[turn, k, :, :, c] = mine
+        for d in range(1, near):
+            near_copy(turn, k, d).start()
+
+    def sum_near(turn, k):
+        for d in range(1, near):
+            near_copy(turn, k, d).wait_recv()
+        mine = parts[turn, k, :, b, c]
+        for d in range(1, near):
+            mine = mine + got_near[turn, k, d - 1]
+        parts[turn, k, :, b, c] = mine
+        for d in range(1, far):
+            far_copy(turn, k, d).start()
+
+    def sum_far(turn, k):
+        for d in range(1, far):
+            far_copy(turn, k, d).wait_recv()
+        mine = parts[turn, k, a, b, c]
+        for d in range(1, far):
+            mine = mine + got_far[turn, k, d - 1]
+        return mine
+
+    def sum_end(turn):
+        for k in range(chunks):
+            for n in range(1, core):
+                core_copy(turn, k, n).wait_send()
+            for n in range(1, near):
+                near_copy(turn, k, n).wait_send()
+            for n in range(1, far):
+                far_copy(turn, k, n).wait_send()
+
+    def matmuls(turn):
+        for k in range(chunks):
+            gather_wait(turn, k, 3)
+            high, low = split(held[turn][k][source].reshape(op * ROWS, width))
+            inner[:, pl.ds(k * ROWS, ROWS), :] = product3(
+                high, low, right_h[...], right_l[...]
+            ).reshape(op, ROWS, width)
+        whole = inner[...].reshape(op * rows, width)
+        high, low = split(whole)
+        inner_h[...] = high
+        inner_l[...] = low
+
+        @pl.loop(0, chunks)
+        def _(k):
+            out = product3(left_h[k], left_l[k], inner_h[...], inner_l[...])
+            parts[turn, k] = out.reshape(far, near, core, ROWS, width)
+            for d in range(1, core):
+                core_copy(turn, k, d).start()
+
+    for k in range(chunks):
+        gather_start(0, k, 0)
+    loads[0].wait()
+    high, low = split(right_f[...])
+    right_h[...] = high
+    right_l[...] = low
+    norm_part = total(raw[...] * raw[...])
+    for k in range(chunks):
+        gather_wait(0, k, 0)
+        gather_start(0, k, 1)
+    loads[1].wait()
+    for k in range(chunks):
+        high, low = split(left_f[:, pl.ds(k * ROWS, ROWS), :].reshape(op * ROWS, width))
+        left_h[k] = high
+        left_l[k] = low
+    for stage in (1, 2):
+        for k in range(chunks):
+            gather_wait(0, k, stage)
+            gather_start(0, k, stage + 1)
+    matmuls(0)
+    along_part = jnp.zeros((1, 1), F32)
+    for k in range(chunks):
+        along_part = along_part + total(held[0][k][y] * parts[0, k])
+        sum_core(0, k)
+    tile_start(0, 0, (norm_part, along_part))
+    for k in range(chunks):
+        sum_near(0, k)
+        if k < 4:
+            tile_advance(0, k)
+    for k in range(min(chunks, 4), 4):
+        tile_advance(0, k)
+
+    norm_raw = tile_read(0, 0)
+    product_raw = tile_read(0, 1)
+    scale = 1.0 / jnp.sqrt(norm_raw + EPS)
+    rayleigh = product_raw / (norm_raw + EPS)
+    along_part = jnp.zeros((1, 1), F32)
+    for k in range(chunks):
+        here = pl.ds(k * ROWS, ROWS)
+        v_zero = scale * raw[here, :]
+        w_zero = scale * (sum_far(0, k) * mask[k * ROWS : (k + 1) * ROWS])
+        update = (w_zero - rayleigh * v_zero) / den_ref[here, :]
+        applied[here, :] = w_zero
+        step[here, :] = update
+        held[1][k][y, a, b, c] = update
+        gather_start(1, k, 0)
+        along_part = along_part + total(v_zero * update)
+
+    tile_start(1, 0, (along_part,))
+    for stage in range(3):
+        for k in range(chunks):
+            gather_wait(1, k, stage)
+            gather_start(1, k, stage + 1)
+        tile_advance(1, stage)
+    tile_advance(1, 3)
+    along = tile_read(1, 0)
+    v_zero = scale * raw[...]
+    update_perp = step[...] - along * v_zero
+    step[...] = update_perp
+    tail_part = total(update_perp * update_perp)
+    couple_part = total(update_perp * applied[...])
+    matmuls(1)
+    corner_part = jnp.zeros((1, 1), F32)
+    shift = along * scale
+    for k in range(chunks):
+        corner_part = corner_part + total((held[1][k][y] - shift * held[0][k][y]) * parts[1, k])
+        sum_core(1, k)
+    tile_start(2, 0, (tail_part, couple_part, corner_part))
+    for k in range(chunks):
+        sum_near(1, k)
+        if k < 4:
+            tile_advance(2, k)
+    for k in range(min(chunks, 4), 4):
+        tile_advance(2, k)
+
+    tail = tile_read(2, 0)
+    perp_w_zero = tile_read(2, 1)
+    perp_w = tile_read(2, 2) - along * perp_w_zero
+    gain = 1.0 / jnp.sqrt(tail + EPS)
+    corner = gain * gain * perp_w
+    couple = gain * perp_w_zero
+    down, across = 2.0 * couple, rayleigh - corner
+    most = jnp.maximum(jnp.abs(down), jnp.abs(across))
+    safe = jnp.where(most > 0.0, most, 1.0)
+    down, across = down / safe, jnp.where(most > 0.0, across / safe, 1.0)
+    length = jnp.sqrt(down * down + across * across)
+    larger = jnp.sqrt(0.5 * (1.0 + jnp.abs(across) / length))
+    smaller = 0.5 * jnp.abs(down) / (length * larger)
+    sign = jnp.where(down < 0.0, -1.0, 1.0)
+    cosine = jnp.where(across >= 0.0, larger, smaller)
+    sine = sign * jnp.where(across >= 0.0, smaller, larger)
+    lam = sine * sine * rayleigh + cosine * cosine * corner - 2.0 * sine * cosine * couple
+    for k in range(chunks):
+        here = pl.ds(k * ROWS, ROWS)
+        w_zero = applied[here, :]
+        w_one = gain * (sum_far(1, k) * mask[k * ROWS : (k + 1) * ROWS] - along * w_zero)
+        new_vector = sine * (scale * raw[here, :]) - cosine * (gain * step[here, :])
+        mixed = sine * w_zero - cosine * w_one
+        new_ref[here, :] = new_vector
+        corr_ref[here, :] = (mixed - lam * new_vector) / den_ref[here, :]
+
+    for turn in range(2):
+        gather_end(turn)
+        sum_end(turn)
+    for red in range(3):
+        for stage, axis in enumerate(("far", "near", "sec", "core")):
+            for d in range(1, size[axis]):
+                tile_copy(red, stage, d).wait_send()
+
+
+def fused(dims, sec, psi, left_env, right_env, denominators, source_sector, owner, orders):
+    rows, _, width = psi.shape
+    far, near, core = dims
+    op = far * near * core
+    chunks = rows // ROWS
+    peers = far + near + core + sec - 4
+    vmem = pl.BlockSpec(memory_space=pltpu.VMEM)
+    smem = pl.BlockSpec(memory_space=pltpu.SMEM)
+    hbm = pl.BlockSpec(memory_space=pl.ANY)
+    block = (ROWS, width)
+    scratch = [pltpu.VMEM((sec, far, near, core) + block, F32)] * (2 * chunks) + [
+        pltpu.VMEM((op, rows, width), F32),
+        pltpu.VMEM((width, width), F32),
+        pltpu.VMEM((chunks, op * ROWS, width), BF16),
+        pltpu.VMEM((chunks, op * ROWS, width), BF16),
+        pltpu.VMEM((width, width), BF16),
+        pltpu.VMEM((width, width), BF16),
+        pltpu.VMEM((op, rows, width), F32),
+        pltpu.VMEM((op * rows, width), BF16),
+        pltpu.VMEM((op * rows, width), BF16),
+        pltpu.VMEM((rows, width), F32),
+        pltpu.VMEM((rows, width), F32),
+        pltpu.VMEM((rows, width), F32),
+        pltpu.VMEM((2, chunks, far, near, core) + block, F32),
+        pltpu.VMEM((2, chunks, core - 1, far, near) + block, F32),
+        pltpu.VMEM((2, chunks, near - 1, far) + block, F32),
+        pltpu.VMEM((2, chunks, far - 1) + block, F32),
+        pltpu.VMEM((3, 5, 8, 128), F32),
+        pltpu.VMEM((3, peers, 8, 128), F32),
+        pltpu.SemaphoreType.DMA((2,)),
+        pltpu.SemaphoreType.DMA((2, chunks, peers)),
+        pltpu.SemaphoreType.DMA((2, chunks, peers)),
+        pltpu.SemaphoreType.DMA((2, chunks, peers)),
+        pltpu.SemaphoreType.DMA((2, chunks, peers)),
+        pltpu.SemaphoreType.DMA((3, peers)),
+        pltpu.SemaphoreType.DMA((3, peers)),
+    ]
+    flat = jax.ShapeDtypeStruct((rows, width), F32)
+    new_vector, correction = pl.pallas_call(
+        functools.partial(kernel, dims, sec),
+        out_shape=(flat, flat),
+        in_specs=[vmem, hbm, hbm, vmem, smem, smem, smem],
+        out_specs=(vmem, vmem),
+        scratch_shapes=scratch,
+        compiler_params=pltpu.CompilerParams(
+            collective_id=0, has_side_effects=True, vmem_limit_bytes=52 * 2**20
+        ),
+    )(
+        psi.reshape(rows, width),
+        left_env.reshape(op, rows, width),
+        right_env.reshape(width, width),
+        denominators.reshape(rows, width),
+        source_sector,
+        owner,
+        orders,
+    )
+    return new_vector.reshape(psi.shape), correction.reshape(psi.shape)
+
+
+def per_device(*arrays):
+    psi, left_env = arrays[0], arrays[1]
+    op = lax.axis_size("op")
+    sec = lax.axis_size("sec")
+    rows, sec_here, width = psi.shape
+    core = 2 if op % 2 == 0 else 1
+    chips = op // core
+    near = max(n for n in range(1, chips + 1) if chips % n == 0 and n * n <= chips)
+    dims = (chips // near, near, core)
+    fits = rows % ROWS == 0 and width % 128 == 0 and left_env.shape[:2] == (1, 1)
+    if fits and sec_here == 1 and min(dims) > 1 and sec > 1 and op * rows == width:
+        return fused(dims, sec, *arrays)
+    return general(*arrays)
+
+
 def solution(mesh):
     placed = (
         P("op", "sec", None),

time: 537 us -> 109 us (0.20)
  blocking collectives: 262 us -> 0 us
  waiting for transfers between devices: 187 us -> 0 us
  Pallas kernels: 0 us -> 104 us
  matrix products: 28.2 us -> 0 us
  between operations: 22.4 us -> 0.65 us
  local copies, waits for them, and re-layouts: 21.1 us -> 4.51 us
  other arithmetic: 15 us -> 0 us
    unnamed x4 -> x0, waiting for transfers between devices: 187 us -> none
    psum x4 -> x0, blocking collectives: 159 us -> none  [the longest x1 40.5 us: per_device(): lax.psum(partial_sum(update_perp, update_perp), ('op', 'sec')) / count]
    pallas_call x0 -> x1, Pallas kernels: none -> 104 us  [fused(): pl.pallas_call(functools.partial(kernel, dims, sec), out_shape=(flat, fla...]
    all_to_all x2 -> x0, blocking collectives: 90.2 us -> none  [apply(): lax.all_to_all(outgoing, 'op', split_axis=1, concat_axis=0, tiled=True)]
    dot_general x4 -> x0, matrix products: 28.2 us -> none  [the longest x2 18.8 us: apply(): product = jnp.einsum('pxa,apc->xpc', left_flat, inner, precision=HIGH)]
    all_gather x2 -> x0, blocking collectives: 12.3 us -> none  [apply(): shard_all = lax.all_gather(vector, 'sec', axis=1, tiled=True)]
    transpose x2 -> x0, local copies, waits for them, and re-layouts: 9 us -> none  [apply(): product = jnp.einsum('pxa,apc->xpc', left_flat, inner, precision=HIGH)]
    reduce_sum x5 -> x0, other arithmetic: 6.4 us -> none  [the longest x4 5.52 us: partial_sum(): return jnp.sum(first * second)]
  transfers between devices with their start and end apart: 2 -> 0, of which waited for: 2 -> 0; matrix products, arithmetic and copies ran while one was open for 0% -> 0% of each run, Pallas kernels for 0% -> 0%
where the time goes in v1:
time: 109 us
  Pallas kernels  104 us (95%)
  local copies, waits for them, and re-layouts  4.51 us (4%)
    pallas_call x1, Pallas kernels, fused(): pl.pallas_call(functools.partial(kernel, dims, sec), out_shape=(flat, fla...  104 us
    unnamed x8, local copies, waits for them, and re-layouts  4.51 us

profile of v1, /device:TPU:0, one launch (start us, length us, event | category | flops | bytes accessed | tf_op | source)
XLA Modules:
  0.0 108.8 jit_solution(7947283858703485386)
XLA Ops:
  0.6 0.8 copy.9.source_ref
  1.4 1.0 copy_bitcast_fusion
  2.3 0.0 copy-start
  2.4 0.6 copy-done
  3.0 0.0 copy-start.1
  3.0 0.7 copy-done.1
  3.7 103.6 %shard_map.86 = (f32[40,640]{1,0:T(8,128)S(1)}, f32[40,640]{1,0:T(8,128)S(1)}) custom-call(f32[40,640]{1,0:T(8,128)S(1)} %get-tuple-element.9.psi_ref, f32[16,40,640]{2,1,0:T(8,128)} %bitcast.10, f32[640,640]{1,0:T(8,128)} %bitcast.11, f32[40,640]{1,0:T(8,128)S(1)} %get-tuple-element.8.den_ref, s32[16,2]{1,0:T(8,128)S(1)} %copy.9.source_ref, s32[2]{0:T(128)S(1)} %copy-done, ...), custom_call_target="tpu_custom_call" | custom-call | tf_op jit(solution)/shard_map/pallas_call | solution.py:474
  107.3 0.7 copy.10
  108.1 0.7 copy.11
Async XLA Ops:
  2.3 0.7 copy-start
  3.0 0.7 copy-start.1

commit v2 on v1

v2 whole, which is shorter than its diff:
```python
import functools

import jax
import jax.numpy as jnp
from jax import lax
from jax.experimental import pallas as pl
from jax.experimental.pallas import tpu as pltpu
from jax.sharding import PartitionSpec as P

EPS = 1e-06
HIGH = lax.Precision.HIGHEST
MESH = pl.DeviceIdType.MESH
F32 = jnp.float32
BF16 = jnp.bfloat16
ROWS = 8


def slot_sectors(owner):
    slots = jnp.arange(owner.shape[0], dtype=jnp.int32)
    hits = (owner[None, :] == slots[:, None]).astype(jnp.int32)
    return jnp.sum(hits * slots[None, :], axis=1)


def general(psi, left_env, right_env, denominators, source_sector, owner, orders):
    rows_here = psi.shape[0]
    sec_here = psi.shape[1]
    width = psi.shape[2]
    term_here = left_env.shape[0]
    op_size = lax.axis_size("op")
    sec_size = lax.axis_size("sec")
    op_pos = lax.axis_index("op")
    sec_pos = lax.axis_index("sec")
    sectors = slot_sectors(owner)
    sectors_here = lax.dynamic_slice_in_dim(sectors, sec_pos * sec_here, sec_here, 0)
    order_here = jnp.take(orders, sectors_here)
    row_ids = op_pos * rows_here + jnp.arange(rows_here, dtype=jnp.int32)
    col_ids = jnp.arange(width, dtype=jnp.int32)
    mask = (
        (row_ids[:, None, None] < order_here[None, :, None])
        & (col_ids[None, None, :] < order_here[None, :, None])
    ).astype(jnp.float32)
    source_all = jnp.take(owner, jnp.take(source_sector, sectors_here, axis=1))
    blocks = term_here * sec_here
    left_flat = left_env.reshape(blocks, width, width)
    right_flat = right_env.reshape(blocks, width, width)
    count = float(rows_here * sec_here * width * op_size * sec_size)

    def apply(vector):
        shard_all = lax.all_gather(vector, "sec", axis=1, tiled=True)
        outgoing = jnp.take(shard_all, source_all.reshape(-1), axis=1).reshape(
            rows_here, op_size, blocks, width
        )
        chosen = lax.all_to_all(outgoing, "op", split_axis=1, concat_axis=0, tiled=True).reshape(
            width, blocks, width
        )
        inner = jnp.einsum("apb,pbc->apc", chosen, right_flat, precision=HIGH)
        product = jnp.einsum("pxa,apc->xpc", left_flat, inner, precision=HIGH)
        whole = product.reshape(width, term_here, sec_here, width).sum(axis=1)
        summed = lax.psum_scatter(whole, "op", scatter_dimension=0, tiled=True)
        return summed * mask

    def partial_sum(first, second):
        return jnp.sum(first * second)

    v_raw = psi * mask
    w_raw = apply(v_raw)
    start_pair = lax.psum(
        jnp.stack([partial_sum(v_raw, v_raw), partial_sum(v_raw, w_raw)]), ("op", "sec")
    )
    norm_raw = start_pair[0] / count
    product_raw = start_pair[1] / count
    scale = 1.0 / jnp.sqrt(norm_raw + EPS)
    v_zero = scale * v_raw
    w_zero = scale * w_raw
    rayleigh = product_raw / (norm_raw + EPS)
    update = (w_zero - rayleigh * v_zero) / denominators
    along = lax.psum(partial_sum(v_zero, update), ("op", "sec")) / count
    update_perp = update - along * v_zero
    tail = lax.psum(partial_sum(update_perp, update_perp), ("op", "sec")) / count
    v_one = update_perp / jnp.sqrt(tail + EPS)
    w_one = apply(v_one)
    sub_pair = lax.psum(
        jnp.stack([partial_sum(v_one, w_one), partial_sum(v_one, w_zero)]), ("op", "sec")
    )
    corner = sub_pair[0] / count
    couple = sub_pair[1] / count
    angle = 0.5 * jnp.arctan2(2.0 * couple, rayleigh - corner)
    sine = jnp.sin(angle)
    cosine = jnp.cos(angle)
    new_vector = sine * v_zero - cosine * v_one
    applied = sine * w_zero - cosine * w_one
    lam = sine * sine * rayleigh + cosine * cosine * corner - 2.0 * sine * cosine * couple
    correction = (applied - lam * new_vector) / denominators
    return (new_vector, correction)


def split(value):
    high = value.astype(BF16)
    return high, (value - high.astype(F32)).astype(BF16)


def product3(ah, al, bh, bl):
    dot = functools.partial(jnp.dot, preferred_element_type=F32)
    return dot(ah, bh) + (dot(ah, bl) + dot(al, bh))


def end_scalars(tile_read, along, rayleigh):
    tail = tile_read(2, 0)
    perp_w_zero = tile_read(2, 1)
    perp_w = tile_read(2, 2) - along * perp_w_zero
    gain = 1.0 / jnp.sqrt(tail + EPS)
    corner = gain * gain * perp_w
    couple = gain * perp_w_zero
    down, across = 2.0 * couple, rayleigh - corner
    most = jnp.maximum(jnp.abs(down), jnp.abs(across))
    safe = jnp.where(most > 0.0, most, 1.0)
    down, across = down / safe, jnp.where(most > 0.0, across / safe, 1.0)
    length = jnp.sqrt(down * down + across * across)
    larger = jnp.sqrt(0.5 * (1.0 + jnp.abs(across) / length))
    smaller = 0.5 * jnp.abs(down) / (length * larger)
    sign = jnp.where(down < 0.0, -1.0, 1.0)
    cosine = jnp.where(across >= 0.0, larger, smaller)
    sine = sign * jnp.where(across >= 0.0, smaller, larger)
    lam = sine * sine * rayleigh + cosine * cosine * corner - 2.0 * sine * cosine * couple
    return gain, sine, cosine, lam


def kernel(
    dims, sec, psi_ref, left_hbm, right_hbm, den_ref, source_ref, owner_ref, orders_ref,
    new_ref, corr_ref, *scratch
):
    far, near, core = dims
    chunks = psi_ref.shape[0] // ROWS
    rows = psi_ref.shape[0]
    width = psi_ref.shape[1]
    op = far * near * core
    held = (scratch[:chunks], scratch[chunks : 2 * chunks])
    (left_f, right_f, left_h, left_l, right_h, right_l, inner, inner_h, inner_l, raw,
     applied, step, parts, got_core, got_near, got_far, tiles, got_tiles, load_sem,
     gather_send, gather_recv, sum_send, sum_recv, tile_send, tile_recv) = scratch[2 * chunks :]

    me = lax.axis_index("op")
    y = lax.axis_index("sec")
    c = lax.rem(me, core)
    b = lax.rem(lax.div(me, core), near)
    a = lax.div(me, core * near)
    where = {"far": a, "near": b, "core": c, "sec": y}
    size = {"far": far, "near": near, "core": core, "sec": sec}

    def turned(axis, by):
        place = dict(where)
        place[axis] = lax.rem(where[axis] + by + size[axis], size[axis])
        return place

    def device(place):
        return ((place["far"] * near + place["near"]) * core + place["core"], place["sec"])

    every = [(axis, d) for axis in ("far", "near", "sec", "core") for d in range(1, size[axis])]
    around = [
        (("near", i), ("core", j), ("sec", l))
        for i in range(near) for j in range(core) for l in range(sec) if i + j + l > 0
    ]
    along_far = [(("far", d),) for d in range(1, far)]

    def moved(offset):
        place = dict(where)
        for axis, by in offset:
            place[axis] = lax.rem(where[axis] + by, size[axis])
        return place

    loads = [
        pltpu.make_async_copy(right_hbm, right_f, load_sem.at[0]),
        pltpu.make_async_copy(left_hbm, left_f, load_sem.at[1]),
    ]
    for load in loads:
        load.start()

    barrier = pltpu.get_barrier_semaphore()
    for offset in around + along_far:
        pl.semaphore_signal(
            barrier, inc=1, device_id=device(moved(offset)), device_id_type=MESH
        )

    sector = jnp.int32(0)
    for s in range(sec):
        sector = sector + jnp.where(owner_ref[s] == y, s, 0)
    order = orders_ref[sector]
    source = owner_ref[source_ref[me, sector]]

    row_ids = lax.broadcasted_iota(jnp.int32, (rows, width), 0) + me * rows
    col_ids = lax.broadcasted_iota(jnp.int32, (rows, width), 1)
    mask = ((row_ids < order) & (col_ids < order)).astype(F32)
    raw[...] = psi_ref[...] * mask
    for k in range(chunks):
        held[0][k][y, a, b, c] = raw[pl.ds(k * ROWS, ROWS), :]

    pl.semaphore_wait(barrier, len(around + along_far))

    def area(axes, place):
        pick = lambda axis: slice(None) if axis in axes else place[axis]
        return (pick("sec"), pick("far"), pick("near"), pick("core"))

    def sequence(k):
        return ("far", "near", "sec", "core") if k % 2 == 0 else ("far", "sec", "near", "core")

    slot_of = {pair: n for n, pair in enumerate(every)}

    def gather_copy(turn, k, stage, d, from_place, to_place):
        axes = sequence(k)
        block = held[turn][k].at[area(axes[:stage], from_place)]
        n = slot_of[(axes[stage], d)]
        return pltpu.make_async_remote_copy(
            src_ref=block, dst_ref=block,
            send_sem=gather_send.at[turn, k, n], recv_sem=gather_recv.at[turn, k, n],
            device_id=device(to_place), device_id_type=MESH,
        )

    def gather_start(turn, k, stage):
        axis = sequence(k)[stage]
        for d in range(1, size[axis]):
            gather_copy(turn, k, stage, d, where, turned(axis, d)).start()

    def gather_wait(turn, k, stage):
        axis = sequence(k)[stage]
        for d in range(1, size[axis]):
            gather_copy(turn, k, stage, d, turned(axis, -d), turned(axis, d)).wait_recv()

    def gather_end(turn):
        for k in range(chunks):
            for stage, axis in enumerate(sequence(k)):
                for d in range(1, size[axis]):
                    gather_copy(turn, k, stage, d, where, turned(axis, d)).wait_send()

    groups = (around, along_far)

    def tile_copy(red, stage, n):
        slot = n + stage * len(around)
        return pltpu.make_async_remote_copy(
            src_ref=tiles.at[red, stage], dst_ref=got_tiles.at[red, slot],
            send_sem=tile_send.at[red, slot], recv_sem=tile_recv.at[red, slot],
            device_id=device(moved(groups[stage][n])), device_id_type=MESH,
        )

    def tile_send_all(red, stage):
        for n in range(len(groups[stage])):
            tile_copy(red, stage, n).start()

    def tile_start(red, values):
        line = lax.broadcasted_iota(jnp.int32, (8, 128), 0)
        tile = jnp.zeros((8, 128), F32)
        for n, value in enumerate(values):
            tile = jnp.where(line == n, value, tile)
        tiles[red, 0] = tile
        tile_send_all(red, 0)

    def tile_advance(red, stage):
        total = tiles[red, stage]
        for n in range(len(groups[stage])):
            tile_copy(red, stage, n).wait_recv()
            total = total + got_tiles[red, n + stage * len(around)]
        tiles[red, stage + 1] = total
        if stage == 0:
            tile_send_all(red, 1)

    count = float(rows * width * op * sec)

    def tile_read(red, n):
        return tiles[red, 2, pl.ds(n, 1), pl.ds(0, 1)] / count

    def total(value):
        return jnp.sum(value.reshape(-1, width), keepdims=True)

    def core_copy(turn, k, d):
        place = turned("core", d)
        return pltpu.make_async_remote_copy(
            src_ref=parts.at[turn, k, :, :, place["core"]], dst_ref=got_core.at[turn, k, d - 1],
            send_sem=sum_send.at[turn, k, slot_of[("core", d)]],
            recv_sem=sum_recv.at[turn, k, slot_of[("core", d)]],
            device_id=device(place), device_id_type=MESH,
        )

    def near_copy(turn, k, d):
        place = turned("near", d)
        return pltpu.make_async_remote_copy(
            src_ref=parts.at[turn, k, :, place["near"], c], dst_ref=got_near.at[turn, k, d - 1],
            send_sem=sum_send.at[turn, k, slot_of[("near", d)]],
            recv_sem=sum_recv.at[turn, k, slot_of[("near", d)]],
            device_id=device(place), device_id_type=MESH,
        )

    def far_copy(turn, k, d):
        place = turned("far", d)
        return pltpu.make_async_remote_copy(
            src_ref=parts.at[turn, k, place["far"], b, c], dst_ref=got_far.at[turn, k, d - 1],
            send_sem=sum_send.at[turn, k, slot_of[("far", d)]],
            recv_sem=sum_recv.at[turn, k, slot_of[("far", d)]],
            device_id=device(place), device_id_type=MESH,
        )

    def sum_core(turn, k):
        for d in range(1, core):
            core_copy(turn, k, d).wait_recv()
        mine = parts[turn, k, :, :, c]
        for d in range(1, core):
            mine = mine + got_core[turn, k, d - 1]
        parts[turn, k, :, :, c] = mine
        for d in range(1, near):
            near_copy(turn, k, d).start()

    def sum_near(turn, k):
        for d in range(1, near):
            near_copy(turn, k, d).wait_recv()
        mine = parts[turn, k, :, b, c]
        for d in range(1, near):
            mine = mine + got_near[turn, k, d - 1]
        parts[turn, k, :, b, c] = mine
        for d in range(1, far):
            far_copy(turn, k, d).start()

    def sum_far(turn, k):
        for d in range(1, far):
            far_copy(turn, k, d).wait_recv()
        mine = parts[turn, k, a, b, c]
        for d in range(1, far):
            mine = mine + got_far[turn, k, d - 1]
        return mine

    def sum_end(turn):
        for k in range(chunks):
            for n in range(1, core):
                core_copy(turn, k, n).wait_send()
            for n in range(1, near):
                near_copy(turn, k, n).wait_send()
            for n in range(1, far):
                far_copy(turn, k, n).wait_send()

    def gather_rest(turn, beside):
        for k in range(chunks + 1):
            if k < chunks:
                gather_wait(turn, k, 0)
                gather_start(turn, k, 1)
                beside(k)
            if k > 0:
                gather_wait(turn, k - 1, 1)
                gather_start(turn, k - 1, 2)

    def matmuls(turn, weigh):
        for k in range(chunks + 1):
            if k < chunks:
                gather_wait(turn, k, 2)
                gather_start(turn, k, 3)
            if k > 0:
                gather_wait(turn, k - 1, 3)
                high, low = split(held[turn][k - 1][source].reshape(op * ROWS, width))
                inner[:, pl.ds((k - 1) * ROWS, ROWS), :] = product3(
                    high, low, right_h[...], right_l[...]
                ).reshape(op, ROWS, width)
        whole = inner[...].reshape(op * rows, width)
        high, low = split(whole)
        inner_h[...] = high
        inner_l[...] = low
        weighed = jnp.zeros((1, 1), F32)
        for k in range(chunks):
            out = product3(left_h[k], left_l[k], inner_h[...], inner_l[...])
            parts[turn, k] = out.reshape(far, near, core, ROWS, width)
            for d in range(1, core):
                core_copy(turn, k, d).start()
            weighed = weighed + total(weigh(k) * parts[turn, k])
            if k > 0:
                sum_core(turn, k - 1)
        sum_core(turn, chunks - 1)
        return weighed

    def finish(turn, red, ready, use):
        values = None
        for k in range(chunks + 2):
            if k < chunks:
                sum_near(turn, k)
            if k < 2:
                tile_advance(red, k)
            else:
                if k == 2:
                    values = ready()
                use(k - 2, values)

    for k in range(chunks):
        gather_start(0, k, 0)
    loads[0].wait()
    high, low = split(right_f[...])
    right_h[...] = high
    right_l[...] = low
    norm_part = total(raw[...] * raw[...])
    loads[1].wait()

    def split_left(k):
        high, low = split(left_f[:, pl.ds(k * ROWS, ROWS), :].reshape(op * ROWS, width))
        left_h[k] = high
        left_l[k] = low

    gather_rest(0, split_left)
    start_part = matmuls(0, lambda k: held[0][k][y])
    tile_start(0, (norm_part, start_part))

    def start_values():
        norm_raw = tile_read(0, 0)
        product_raw = tile_read(0, 1)
        return 1.0 / jnp.sqrt(norm_raw + EPS), product_raw / (norm_raw + EPS)

    kept = {"along": jnp.zeros((1, 1), F32)}

    def take_step(k, values):
        scale, rayleigh = values
        kept["scale"], kept["rayleigh"] = values
        here = pl.ds(k * ROWS, ROWS)
        v_zero = scale * raw[here, :]
        w_zero = scale * (sum_far(0, k) * mask[k * ROWS : (k + 1) * ROWS])
        update = (w_zero - rayleigh * v_zero) / den_ref[here, :]
        applied[here, :] = w_zero
        step[here, :] = update
        held[1][k][y, a, b, c] = update
        gather_start(1, k, 0)
        kept["along"] = kept["along"] + total(v_zero * update)

    finish(0, 0, start_values, take_step)
    scale, rayleigh = kept["scale"], kept["rayleigh"]

    tile_start(1, (kept["along"],))

    def sum_along(k):
        if k in (1, 3):
            tile_advance(1, k // 2)

    gather_rest(1, sum_along)
    for stage in range(2):
        if 2 * stage + 1 >= chunks:
            tile_advance(1, stage)
    along = tile_read(1, 0)
    v_zero = scale * raw[...]
    update_perp = step[...] - along * v_zero
    step[...] = update_perp
    tail_part = total(update_perp * update_perp)
    couple_part = total(update_perp * applied[...])
    shift = along * scale
    corner_part = matmuls(1, lambda k: held[1][k][y] - shift * held[0][k][y])
    tile_start(2, (tail_part, couple_part, corner_part))

    def end_values():
        return end_scalars(tile_read, along, rayleigh)

    def give(k, values):
        gain, sine, cosine, lam = values
        here = pl.ds(k * ROWS, ROWS)
        w_zero = applied[here, :]
        w_one = gain * (sum_far(1, k) * mask[k * ROWS : (k + 1) * ROWS] - along * w_zero)
        new_vector = sine * (scale * raw[here, :]) - cosine * (gain * step[here, :])
        mixed = sine * w_zero - cosine * w_one
        new_ref[here, :] = new_vector
        corr_ref[here, :] = (mixed - lam * new_vector) / den_ref[here, :]

    finish(1, 2, end_values, give)

    for turn in range(2):
        gather_end(turn)
        sum_end(turn)
    for red in range(3):
        for stage in range(2):
            for n in range(len(groups[stage])):
                tile_copy(red, stage, n).wait_send()


def fused(dims, sec, psi, left_env, right_env, denominators, source_sector, owner, orders):
    rows, _, width = psi.shape
    far, near, core = dims
    op = far * near * core
    chunks = rows // ROWS
    peers = far + near + core + sec - 4
    pairs = near * core * sec - 1 + far - 1
    vmem = pl.BlockSpec(memory_space=pltpu.VMEM)
    smem = pl.BlockSpec(memory_space=pltpu.SMEM)
    hbm = pl.BlockSpec(memory_space=pl.ANY)
    block = (ROWS, width)
    scratch = [pltpu.VMEM((sec, far, near, core) + block, F32)] * (2 * chunks) + [
        pltpu.VMEM((op, rows, width), F32),
        pltpu.VMEM((width, width), F32),
        pltpu.VMEM((chunks, op * ROWS, width), BF16),
        pltpu.VMEM((chunks, op * ROWS, width), BF16),
        pltpu.VMEM((width, width), BF16),
        pltpu.VMEM((width, width), BF16),
        pltpu.VMEM((op, rows, width), F32),
        pltpu.VMEM((op * rows, width), BF16),
        pltpu.VMEM((op * rows, width), BF16),
        pltpu.VMEM((rows, width), F32),
        pltpu.VMEM((rows, width), F32),
        pltpu.VMEM((rows, width), F32),
        pltpu.VMEM((2, chunks, far, near, core) + block, F32),
        pltpu.VMEM((2, chunks, core - 1, far, near) + block, F32),
        pltpu.VMEM((2, chunks, near - 1, far) + block, F32),
        pltpu.VMEM((2, chunks, far - 1) + block, F32),
        pltpu.VMEM((3, 3, 8, 128), F32),
        pltpu.VMEM((3, pairs, 8, 128), F32),
        pltpu.SemaphoreType.DMA((2,)),
        pltpu.SemaphoreType.DMA((2, chunks, peers)),
        pltpu.SemaphoreType.DMA((2, chunks, peers)),
        pltpu.SemaphoreType.DMA((2, chunks, peers)),
        pltpu.SemaphoreType.DMA((2, chunks, peers)),
        pltpu.SemaphoreType.DMA((3, pairs)),
        pltpu.SemaphoreType.DMA((3, pairs)),
    ]
    flat = jax.ShapeDtypeStruct((rows, width), F32)
    new_vector, correction = pl.pallas_call(
        functools.partial(kernel, dims, sec),
        out_shape=(flat, flat),
        in_specs=[vmem, hbm, hbm, vmem, smem, smem, smem],
        out_specs=(vmem, vmem),
        scratch_shapes=scratch,
        compiler_params=pltpu.CompilerParams(
            collective_id=0, has_side_effects=True, vmem_limit_bytes=52 * 2**20
        ),
    )(
        psi.reshape(rows, width),
        left_env.reshape(op, rows, width),
        right_env.reshape(width, width),
        denominators.reshape(rows, width),
        source_sector,
        owner,
        orders,
    )
    return new_vector.reshape(psi.shape), correction.reshape(psi.shape)


def per_device(*arrays):
    psi, left_env = arrays[0], arrays[1]
    op = lax.axis_size("op")
    sec = lax.axis_size("sec")
    rows, sec_here, width = psi.shape
    core = 2 if op % 2 == 0 else 1
    chips = op // core
    near = max(n for n in range(1, chips + 1) if chips % n == 0 and n * n <= chips)
    dims = (chips // near, near, core)
    fits = rows % ROWS == 0 and width % 128 == 0 and left_env.shape[:2] == (1, 1)
    if fits and sec_here == 1 and min(dims) > 1 and sec > 1 and op * rows == width:
        return fused(dims, sec, *arrays)
    return general(*arrays)


def solution(mesh):
    placed = (
        P("op", "sec", None),
        P("op", "sec", None, None),
        P("op", "sec", None, None),
        P("op", "sec", None),
        P(),
        P(),
        P(),
    )
    return jax.shard_map(
        per_device,
        mesh=mesh,
        in_specs=placed,
        out_specs=(P("op", "sec", None), P("op", "sec", None)),
        check_vma=False,
    )
```

time: 109 us -> 111 us (1.018)
    pallas_call x1, Pallas kernels: 104 us -> 105 us  [fused(): pl.pallas_call(functools.partial(kernel, dims, sec), out_shape=(flat, fla...]
where the time goes in v2:
time: 111 us; the launch traced here: 110 us
  Pallas kernels  105 us (95%)
  local copies, waits for them, and re-layouts  4.51 us (4%)
    pallas_call x1, Pallas kernels, fused(): pl.pallas_call(functools.partial(kernel, dims, sec), out_shape=(flat, fla...  105 us
    unnamed x8, local copies, waits for them, and re-layouts  4.51 us

profile of v2, /device:TPU:0, one launch (start us, length us, event | category | flops | bytes accessed | tf_op | source)
XLA Modules:
  0.0 110.5 jit_solution(2279811855117248294)
XLA Ops:
  0.6 0.8 copy.9.source_ref
  1.4 1.0 copy_bitcast_fusion
  2.3 0.0 copy-start
  2.4 0.6 copy-done
  3.0 0.0 copy-start.1
  3.0 0.7 copy-done.1
  3.7 105.3 %shard_map.86 = (f32[40,640]{1,0:T(8,128)S(1)}, f32[40,640]{1,0:T(8,128)S(1)}) custom-call(f32[40,640]{1,0:T(8,128)S(1)} %get-tuple-element.9.psi_ref, f32[16,40,640]{2,1,0:T(8,128)} %bitcast.10, f32[640,640]{1,0:T(8,128)} %bitcast.11, f32[40,640]{1,0:T(8,128)S(1)} %get-tuple-element.8.den_ref, s32[16,2]{1,0:T(8,128)S(1)} %copy.9.source_ref, s32[2]{0:T(128)S(1)} %copy-done, ...), custom_call_target="tpu_custom_call" | custom-call | tf_op jit(solution)/shard_map/pallas_call | solution.py:510
  109.0 0.7 copy.10
  109.7 0.7 copy.11
Async XLA Ops:
  2.3 0.7 copy-start
  3.0 0.7 copy-start.1

commit v3 on v2

--- a/solution.py
+++ b/solution.py
@@ -126,17 +126,17 @@
 
 
 def kernel(
-    dims, sec, psi_ref, left_hbm, right_hbm, den_ref, source_ref, owner_ref, orders_ref,
+    dims, sec, psi_hbm, left_hbm, right_hbm, den_hbm, source_ref, owner_ref, orders_ref,
     new_ref, corr_ref, *scratch
 ):
     far, near, core = dims
-    chunks = psi_ref.shape[0] // ROWS
-    rows = psi_ref.shape[0]
-    width = psi_ref.shape[1]
+    chunks = psi_hbm.shape[0] // ROWS
+    rows = psi_hbm.shape[0]
+    width = psi_hbm.shape[2]
     op = far * near * core
     held = (scratch[:chunks], scratch[chunks : 2 * chunks])
     (left_f, right_f, left_h, left_l, right_h, right_l, inner, inner_h, inner_l, raw,
-     applied, step, parts, got_core, got_near, got_far, tiles, got_tiles, load_sem,
+     applied, step, parts, got_core, got_near, got_far, picked, got_picked, chosen, psi_v, den_v, tiles, got_tiles, load_sem,
      gather_send, gather_recv, sum_send, sum_recv, tile_send, tile_recv) = scratch[2 * chunks :]
 
     me = lax.axis_index("op")
@@ -171,9 +171,11 @@
     loads = [
         pltpu.make_async_copy(right_hbm, right_f, load_sem.at[0]),
         pltpu.make_async_copy(left_hbm, left_f, load_sem.at[1]),
+        pltpu.make_async_copy(psi_hbm.at[:, 0], psi_v, load_sem.at[2]),
+        pltpu.make_async_copy(den_hbm.at[:, 0], den_v, load_sem.at[3]),
     ]
-    for load in loads:
-        load.start()
+    for n in (2, 0, 1, 3):
+        loads[n].start()
 
     barrier = pltpu.get_barrier_semaphore()
     for offset in around + along_far:
@@ -190,18 +192,19 @@
     row_ids = lax.broadcasted_iota(jnp.int32, (rows, width), 0) + me * rows
     col_ids = lax.broadcasted_iota(jnp.int32, (rows, width), 1)
     mask = ((row_ids < order) & (col_ids < order)).astype(F32)
-    raw[...] = psi_ref[...] * mask
+    loads[2].wait()
+    raw[...] = psi_v[...] * mask
     for k in range(chunks):
-        held[0][k][y, a, b, c] = raw[pl.ds(k * ROWS, ROWS), :]
+        held[0][k][y, a, b] = raw[pl.ds(k * ROWS, ROWS), :]
 
     pl.semaphore_wait(barrier, len(around + along_far))
 
     def area(axes, place):
         pick = lambda axis: slice(None) if axis in axes else place[axis]
-        return (pick("sec"), pick("far"), pick("near"), pick("core"))
+        return (pick("sec"), pick("far"), pick("near"))
 
     def sequence(k):
-        return ("far", "near", "sec", "core") if k % 2 == 0 else ("far", "sec", "near", "core")
+        return ("far", "near", "sec") if k % 2 == 0 else ("far", "sec", "near")
 
     slot_of = {pair: n for n, pair in enumerate(every)}
 
@@ -225,8 +228,30 @@
         for d in range(1, size[axis]):
             gather_copy(turn, k, stage, d, turned(axis, -d), turned(axis, d)).wait_recv()
 
+    def pick_copy(turn, k, d):
+        n = slot_of[("core", d)]
+        return pltpu.make_async_remote_copy(
+            src_ref=picked.at[turn, k, d - 1], dst_ref=got_picked.at[turn, k, d - 1],
+            send_sem=gather_send.at[turn, k, n], recv_sem=gather_recv.at[turn, k, n],
+            device_id=device(turned("core", d)), device_id_type=MESH,
+        )
+
+    def pick_start(turn, k):
+        for d in range(1, core):
+            term = me - c + lax.rem(c + d, core)
+            picked[turn, k, d - 1] = held[turn][k][owner_ref[source_ref[term, sector]]]
+            pick_copy(turn, k, d).start()
+
+    def pick_wait(turn, k):
+        chosen[:, :, c] = held[turn][k][source]
+        for d in range(1, core):
+            pick_copy(turn, k, d).wait_recv()
+            chosen[:, :, lax.rem(c + core - d, core)] = got_picked[turn, k, d - 1]
+
     def gather_end(turn):
         for k in range(chunks):
+            for d in range(1, core):
+                pick_copy(turn, k, d).wait_send()
             for stage, axis in enumerate(sequence(k)):
                 for d in range(1, size[axis]):
                     gather_copy(turn, k, stage, d, where, turned(axis, d)).wait_send()
@@ -306,6 +331,7 @@
         parts[turn, k, :, :, c] = mine
         for d in range(1, near):
             near_copy(turn, k, d).start()
+        return mine
 
     def sum_near(turn, k):
         for d in range(1, near):
@@ -348,10 +374,10 @@
         for k in range(chunks + 1):
             if k < chunks:
                 gather_wait(turn, k, 2)
-                gather_start(turn, k, 3)
+                pick_start(turn, k)
             if k > 0:
-                gather_wait(turn, k - 1, 3)
-                high, low = split(held[turn][k - 1][source].reshape(op * ROWS, width))
+                pick_wait(turn, k - 1)
+                high, low = split(chosen[...].reshape(op * ROWS, width))
                 inner[:, pl.ds((k - 1) * ROWS, ROWS), :] = product3(
                     high, low, right_h[...], right_l[...]
                 ).reshape(op, ROWS, width)
@@ -365,11 +391,9 @@
             parts[turn, k] = out.reshape(far, near, core, ROWS, width)
             for d in range(1, core):
                 core_copy(turn, k, d).start()
-            weighed = weighed + total(weigh(k) * parts[turn, k])
             if k > 0:
-                sum_core(turn, k - 1)
-        sum_core(turn, chunks - 1)
-        return weighed
+                weighed = weighed + total(weigh(k - 1) * sum_core(turn, k - 1))
+        return weighed + total(weigh(chunks - 1) * sum_core(turn, chunks - 1))
 
     def finish(turn, red, ready, use):
         values = None
@@ -391,6 +415,7 @@
     right_l[...] = low
     norm_part = total(raw[...] * raw[...])
     loads[1].wait()
+    loads[3].wait()
 
     def split_left(k):
         high, low = split(left_f[:, pl.ds(k * ROWS, ROWS), :].reshape(op * ROWS, width))
@@ -414,10 +439,10 @@
         here = pl.ds(k * ROWS, ROWS)
         v_zero = scale * raw[here, :]
         w_zero = scale * (sum_far(0, k) * mask[k * ROWS : (k + 1) * ROWS])
-        update = (w_zero - rayleigh * v_zero) / den_ref[here, :]
+        update = (w_zero - rayleigh * v_zero) / den_v[here, :]
         applied[here, :] = w_zero
         step[here, :] = update
-        held[1][k][y, a, b, c] = update
+        held[1][k][y, a, b] = update
         gather_start(1, k, 0)
         kept["along"] = kept["along"] + total(v_zero * update)
 
@@ -455,7 +480,7 @@
         new_vector = sine * (scale * raw[here, :]) - cosine * (gain * step[here, :])
         mixed = sine * w_zero - cosine * w_one
         new_ref[here, :] = new_vector
-        corr_ref[here, :] = (mixed - lam * new_vector) / den_ref[here, :]
+        corr_ref[here, :] = (mixed - lam * new_vector) / den_v[here, :]
 
     finish(1, 2, end_values, give)
 
@@ -479,7 +504,7 @@
     smem = pl.BlockSpec(memory_space=pltpu.SMEM)
     hbm = pl.BlockSpec(memory_space=pl.ANY)
     block = (ROWS, width)
-    scratch = [pltpu.VMEM((sec, far, near, core) + block, F32)] * (2 * chunks) + [
+    scratch = [pltpu.VMEM((sec, far, near) + block, F32)] * (2 * chunks) + [
         pltpu.VMEM((op, rows, width), F32),
         pltpu.VMEM((width, width), F32),
         pltpu.VMEM((chunks, op * ROWS, width), BF16),
@@ -496,9 +521,14 @@
         pltpu.VMEM((2, chunks, core - 1, far, near) + block, F32),
         pltpu.VMEM((2, chunks, near - 1, far) + block, F32),
         pltpu.VMEM((2, chunks, far - 1) + block, F32),
+        pltpu.VMEM((2, chunks, core - 1, far, near) + block, F32),
+        pltpu.VMEM((2, chunks, core - 1, far, near) + block, F32),
+        pltpu.VMEM((far, near, core) + block, F32),
+        pltpu.VMEM((rows, width), F32),
+        pltpu.VMEM((rows, width), F32),
         pltpu.VMEM((3, 3, 8, 128), F32),
         pltpu.VMEM((3, pairs, 8, 128), F32),
-        pltpu.SemaphoreType.DMA((2,)),
+        pltpu.SemaphoreType.DMA((4,)),
         pltpu.SemaphoreType.DMA((2, chunks, peers)),
         pltpu.SemaphoreType.DMA((2, chunks, peers)),
         pltpu.SemaphoreType.DMA((2, chunks, peers)),
@@ -510,17 +540,17 @@
     new_vector, correction = pl.pallas_call(
         functools.partial(kernel, dims, sec),
         out_shape=(flat, flat),
-        in_specs=[vmem, hbm, hbm, vmem, smem, smem, smem],
+        in_specs=[hbm, hbm, hbm, hbm, smem, smem, smem],
         out_specs=(vmem, vmem),
         scratch_shapes=scratch,
         compiler_params=pltpu.CompilerParams(
             collective_id=0, has_side_effects=True, vmem_limit_bytes=52 * 2**20
         ),
     )(
-        psi.reshape(rows, width),
+        psi,
         left_env.reshape(op, rows, width),
         right_env.reshape(width, width),
-        denominators.reshape(rows, width),
+        denominators,
         source_sector,
         owner,
         orders,

time: 111 us -> 111 us (level)
    unnamed x8 -> x11, local copies, waits for them, and re-layouts: 4.51 us -> 5.35 us
where the time goes in v3:
time: 111 us
  Pallas kernels  105 us (95%)
  local copies, waits for them, and re-layouts  5.35 us (5%)
    pallas_call x1, Pallas kernels, fused(): pl.pallas_call(functools.partial(kernel, dims, sec), out_shape=(flat, fla...  105 us
    unnamed x11, local copies, waits for them, and re-layouts  5.35 us

profile of v3, /device:TPU:0, one launch (start us, length us, event | category | flops | bytes accessed | tf_op | source)
XLA Modules:
  0.0 110.5 jit_solution(1561885586972112430)
XLA Ops:
  0.6 0.8 copy.9.source_ref
  1.4 0.0 copy-start
  1.4 0.9 copy-done
  2.3 0.0 copy-start.1
  2.3 0.9 copy-done.1
  3.2 0.0 copy-start.2
  3.2 0.7 copy-done.2
  3.8 0.0 copy-start.3
  3.8 0.7 copy-done.3
  4.5 104.5 %shard_map.86 = (f32[40,640]{1,0:T(8,128)S(1)}, f32[40,640]{1,0:T(8,128)S(1)}) custom-call(f32[40,1,640]{2,1,0:T(1,128)S(1)} %copy-done, f32[16,40,640]{2,1,0:T(8,128)} %bitcast.6, f32[640,640]{1,0:T(8,128)} %bitcast.7, f32[40,1,640]{2,1,0:T(1,128)S(1)} %copy-done.1, s32[16,2]{1,0:T(8,128)S(1)} %copy.9.source_ref, s32[2]{0:T(128)S(1)} %copy-done.2, ...), custom_call_target="tpu_custom_call" | custom-call | tf_op jit(solution)/shard_map/pallas_call | solution.py:540
  109.0 0.7 copy.10
  109.8 0.7 copy.11
Async XLA Ops:
  1.4 0.9 copy-start
  2.3 0.9 copy-start.1
  3.2 0.7 copy-start.2
  3.8 0.7 copy-start.3

commit v4 on v3

--- a/solution.py
+++ b/solution.py
@@ -204,6 +204,8 @@
         return (pick("sec"), pick("far"), pick("near"))
 
     def sequence(k):
+        if k % 5 == 4:
+            return ("near", "sec", "far")
         return ("far", "near", "sec") if k % 2 == 0 else ("far", "sec", "near")
 
     slot_of = {pair: n for n, pair in enumerate(every)}
@@ -304,21 +306,23 @@
             device_id=device(place), device_id_type=MESH,
         )
 
-    def near_copy(turn, k, d):
-        place = turned("near", d)
+    def sum_axes(k):
+        return ("near", "far") if k % 2 == 0 else ("far", "near")
+
+    def sum_copy(turn, k, stage, d):
+        axis = sum_axes(k)[stage]
+        place = turned(axis, d)
+        if axis == "near":
+            row = slice(None) if stage == 0 else a
+            source_ref, target_ref = parts.at[turn, k, row, place["near"], c], got_near
+        else:
+            row = slice(None) if stage == 0 else b
+            source_ref, target_ref = parts.at[turn, k, place["far"], row, c], got_far
+        target = (turn, k, d - 1) if stage == 0 else (turn, k, d - 1, 0)
         return pltpu.make_async_remote_copy(
-            src_ref=parts.at[turn, k, :, place["near"], c], dst_ref=got_near.at[turn, k, d - 1],
-            send_sem=sum_send.at[turn, k, slot_of[("near", d)]],
-            recv_sem=sum_recv.at[turn, k, slot_of[("near", d)]],
-            device_id=device(place), device_id_type=MESH,
-        )
-
-    def far_copy(turn, k, d):
-        place = turned("far", d)
-        return pltpu.make_async_remote_copy(
-            src_ref=parts.at[turn, k, place["far"], b, c], dst_ref=got_far.at[turn, k, d - 1],
-            send_sem=sum_send.at[turn, k, slot_of[("far", d)]],
-            recv_sem=sum_recv.at[turn, k, slot_of[("far", d)]],
+            src_ref=source_ref, dst_ref=target_ref.at[target],
+            send_sem=sum_send.at[turn, k, slot_of[(axis, d)]],
+            recv_sem=sum_recv.at[turn, k, slot_of[(axis, d)]],
             device_id=device(place), device_id_type=MESH,
         )
 
@@ -329,36 +333,38 @@
         for d in range(1, core):
             mine = mine + got_core[turn, k, d - 1]
         parts[turn, k, :, :, c] = mine
-        for d in range(1, near):
-            near_copy(turn, k, d).start()
+        for d in range(1, size[sum_axes(k)[0]]):
+            sum_copy(turn, k, 0, d).start()
         return mine
 
-    def sum_near(turn, k):
-        for d in range(1, near):
-            near_copy(turn, k, d).wait_recv()
-        mine = parts[turn, k, :, b, c]
-        for d in range(1, near):
-            mine = mine + got_near[turn, k, d - 1]
-        parts[turn, k, :, b, c] = mine
-        for d in range(1, far):
-            far_copy(turn, k, d).start()
-
-    def sum_far(turn, k):
-        for d in range(1, far):
-            far_copy(turn, k, d).wait_recv()
+    def sum_first(turn, k):
+        first, second = sum_axes(k)
+        got = got_near if first == "near" else got_far
+        index = (turn, k, slice(None), b, c) if first == "near" else (turn, k, a, slice(None), c)
+        mine = parts[index]
+        for d in range(1, size[first]):
+            sum_copy(turn, k, 0, d).wait_recv()
+            mine = mine + got[turn, k, d - 1]
+        parts[index] = mine
+        for d in range(1, size[second]):
+            sum_copy(turn, k, 1, d).start()
+
+    def sum_second(turn, k):
+        second = sum_axes(k)[1]
+        got = got_near if second == "near" else got_far
         mine = parts[turn, k, a, b, c]
-        for d in range(1, far):
-            mine = mine + got_far[turn, k, d - 1]
+        for d in range(1, size[second]):
+            sum_copy(turn, k, 1, d).wait_recv()
+            mine = mine + got[turn, k, d - 1, 0]
         return mine
 
     def sum_end(turn):
         for k in range(chunks):
             for n in range(1, core):
                 core_copy(turn, k, n).wait_send()
-            for n in range(1, near):
-                near_copy(turn, k, n).wait_send()
-            for n in range(1, far):
-                far_copy(turn, k, n).wait_send()
+            for stage, axis in enumerate(sum_axes(k)):
+                for n in range(1, size[axis]):
+                    sum_copy(turn, k, stage, n).wait_send()
 
     def gather_rest(turn, beside):
         for k in range(chunks + 1):
@@ -399,7 +405,7 @@
         values = None
         for k in range(chunks + 2):
             if k < chunks:
-                sum_near(turn, k)
+                sum_first(turn, k)
             if k < 2:
                 tile_advance(red, k)
             else:
@@ -438,7 +444,7 @@
         kept["scale"], kept["rayleigh"] = values
         here = pl.ds(k * ROWS, ROWS)
         v_zero = scale * raw[here, :]
-        w_zero = scale * (sum_far(0, k) * mask[k * ROWS : (k + 1) * ROWS])
+        w_zero = scale * (sum_second(0, k) * mask[k * ROWS : (k + 1) * ROWS])
         update = (w_zero - rayleigh * v_zero) / den_v[here, :]
         applied[here, :] = w_zero
         step[here, :] = update
@@ -476,7 +482,7 @@
         gain, sine, cosine, lam = values
         here = pl.ds(k * ROWS, ROWS)
         w_zero = applied[here, :]
-        w_one = gain * (sum_far(1, k) * mask[k * ROWS : (k + 1) * ROWS] - along * w_zero)
+        w_one = gain * (sum_second(1, k) * mask[k * ROWS : (k + 1) * ROWS] - along * w_zero)
         new_vector = sine * (scale * raw[here, :]) - cosine * (gain * step[here, :])
         mixed = sine * w_zero - cosine * w_one
         new_ref[here, :] = new_vector
@@ -520,7 +526,7 @@
         pltpu.VMEM((2, chunks, far, near, core) + block, F32),
         pltpu.VMEM((2, chunks, core - 1, far, near) + block, F32),
         pltpu.VMEM((2, chunks, near - 1, far) + block, F32),
-        pltpu.VMEM((2, chunks, far - 1) + block, F32),
+        pltpu.VMEM((2, chunks, far - 1, near) + block, F32),
         pltpu.VMEM((2, chunks, core - 1, far, near) + block, F32),
         pltpu.VMEM((2, chunks, core - 1, far, near) + block, F32),
         pltpu.VMEM((far, near, core) + block, F32),

time: 111 us -> 110 us (level)
  no operation moved by 1% of the time
where the time goes in v4:
time: 110 us
  Pallas kernels  104 us (95%)
  local copies, waits for them, and re-layouts  5.35 us (5%)
    pallas_call x1, Pallas kernels, fused(): pl.pallas_call(functools.partial(kernel, dims, sec), out_shape=(flat, fla...  104 us
    unnamed x11, local copies, waits for them, and re-layouts  5.35 us

profile of v4, /device:TPU:0, one launch (start us, length us, event | category | flops | bytes accessed | tf_op | source)
XLA Modules:
  0.0 109.9 jit_solution(6134633028561445421)
XLA Ops:
  0.6 0.8 copy.9.source_ref
  1.4 0.0 copy-start
  1.4 0.9 copy-done
  2.3 0.0 copy-start.1
  2.3 0.9 copy-done.1
  3.2 0.0 copy-start.2
  3.2 0.7 copy-done.2
  3.8 0.0 copy-start.3
  3.8 0.7 copy-done.3
  4.5 103.9 %shard_map.86 = (f32[40,640]{1,0:T(8,128)S(1)}, f32[40,640]{1,0:T(8,128)S(1)}) custom-call(f32[40,1,640]{2,1,0:T(1,128)S(1)} %copy-done, f32[16,40,640]{2,1,0:T(8,128)} %bitcast.6, f32[640,640]{1,0:T(8,128)} %bitcast.7, f32[40,1,640]{2,1,0:T(1,128)S(1)} %copy-done.1, s32[16,2]{1,0:T(8,128)S(1)} %copy.9.source_ref, s32[2]{0:T(128)S(1)} %copy-done.2, ...), custom_call_target="tpu_custom_call" | custom-call | tf_op jit(solution)/shard_map/pallas_call | solution.py:546
  108.4 0.7 copy.10
  109.2 0.7 copy.11
Async XLA Ops:
  1.4 0.9 copy-start
  2.3 0.9 copy-start.1
  3.2 0.7 copy-start.2
  3.8 0.7 copy-start.3

commit v5 on v4

--- a/solution.py
+++ b/solution.py
@@ -13,6 +13,7 @@
 F32 = jnp.float32
 BF16 = jnp.bfloat16
 ROWS = 8
+TILE = 256
 
 
 def slot_sectors(owner):
@@ -135,7 +136,7 @@
     width = psi_hbm.shape[2]
     op = far * near * core
     held = (scratch[:chunks], scratch[chunks : 2 * chunks])
-    (left_f, right_f, left_h, left_l, right_h, right_l, inner, inner_h, inner_l, raw,
+    (left_f, right_f, left_h, left_l, right_h, right_l, inner, vector_h, vector_l, inner_h, inner_l, raw,
      applied, step, parts, got_core, got_near, got_far, picked, got_picked, chosen, psi_v, den_v, tiles, got_tiles, load_sem,
      gather_send, gather_recv, sum_send, sum_recv, tile_send, tile_recv) = scratch[2 * chunks :]
 
@@ -376,6 +377,8 @@
                 gather_wait(turn, k - 1, 1)
                 gather_start(turn, k - 1, 2)
 
+    tiles_n = [(n, min(TILE, width - n)) for n in range(0, width, TILE)]
+
     def matmuls(turn, weigh):
         for k in range(chunks + 1):
             if k < chunks:
@@ -384,22 +387,33 @@
             if k > 0:
                 pick_wait(turn, k - 1)
                 high, low = split(chosen[...].reshape(op * ROWS, width))
-                inner[:, pl.ds((k - 1) * ROWS, ROWS), :] = product3(
-                    high, low, right_h[...], right_l[...]
-                ).reshape(op, ROWS, width)
-        whole = inner[...].reshape(op * rows, width)
-        high, low = split(whole)
-        inner_h[...] = high
-        inner_l[...] = low
+                vector_h[k - 1] = high
+                vector_l[k - 1] = low
+        full = (op * rows, width)
+        for start, wide in tiles_n:
+            cols = pl.ds(start, wide)
+            out = product3(
+                vector_h[...].reshape(full), vector_l[...].reshape(full),
+                right_h[:, cols], right_l[:, cols],
+            ).reshape(chunks, op, ROWS, wide)
+            for k in range(chunks):
+                inner[:, pl.ds(k * ROWS, ROWS), :wide] = out[k]
+            high, low = split(inner[:, :, :wide].reshape(op * rows, wide))
+            inner_h[:, cols] = high
+            inner_l[:, cols] = low
+        for start, wide in tiles_n:
+            cols = pl.ds(start, wide)
+            parts[turn, :, :, :, :, :, cols] = product3(
+                left_h[...].reshape(full), left_l[...].reshape(full),
+                inner_h[:, cols], inner_l[:, cols],
+            ).reshape(chunks, far, near, core, ROWS, wide)
+        for k in range(chunks):
+            for d in range(1, core):
+                core_copy(turn, k, d).start()
         weighed = jnp.zeros((1, 1), F32)
         for k in range(chunks):
-            out = product3(left_h[k], left_l[k], inner_h[...], inner_l[...])
-            parts[turn, k] = out.reshape(far, near, core, ROWS, width)
-            for d in range(1, core):
-                core_copy(turn, k, d).start()
-            if k > 0:
-                weighed = weighed + total(weigh(k - 1) * sum_core(turn, k - 1))
-        return weighed + total(weigh(chunks - 1) * sum_core(turn, chunks - 1))
+            weighed = weighed + total(weigh(k) * sum_core(turn, k))
+        return weighed
 
     def finish(turn, red, ready, use):
         values = None
@@ -517,7 +531,9 @@
         pltpu.VMEM((chunks, op * ROWS, width), BF16),
         pltpu.VMEM((width, width), BF16),
         pltpu.VMEM((width, width), BF16),
-        pltpu.VMEM((op, rows, width), F32),
+        pltpu.VMEM((op, rows, min(TILE, width)), F32),
+        pltpu.VMEM((chunks, op * ROWS, width), BF16),
+        pltpu.VMEM((chunks, op * ROWS, width), BF16),
         pltpu.VMEM((op * rows, width), BF16),
         pltpu.VMEM((op * rows, width), BF16),
         pltpu.VMEM((rows, width), F32),

time: 110 us -> 114 us (1.036)
  Pallas kernels: 104 us -> 108 us
    pallas_call x1, Pallas kernels: 104 us -> 108 us  [fused(): pl.pallas_call(functools.partial(kernel, dims, sec), out_shape=(flat, fla...]
where the time goes in v5:
time: 114 us
  Pallas kernels  108 us (95%)
  local copies, waits for them, and re-layouts  5.35 us (5%)
    pallas_call x1, Pallas kernels, fused(): pl.pallas_call(functools.partial(kernel, dims, sec), out_shape=(flat, fla...  108 us
    unnamed x11, local copies, waits for them, and re-layouts  5.35 us

profile of v5, /device:TPU:0, one launch (start us, length us, event | category | flops | bytes accessed | tf_op | source)
XLA Modules:
  0.0 114.2 jit_solution(10499349987294791058)
XLA Ops:
  0.6 0.8 copy.9.source_ref
  1.4 0.0 copy-start
  1.4 0.9 copy-done
  2.3 0.0 copy-start.1
  2.3 0.9 copy-done.1
  3.2 0.0 copy-start.2
  3.2 0.7 copy-done.2
  3.8 0.0 copy-start.3
  3.8 0.7 copy-done.3
  4.5 108.3 %shard_map.86 = (f32[40,640]{1,0:T(8,128)S(1)}, f32[40,640]{1,0:T(8,128)S(1)}) custom-call(f32[40,1,640]{2,1,0:T(1,128)S(1)} %copy-done, f32[16,40,640]{2,1,0:T(8,128)} %bitcast.6, f32[640,640]{1,0:T(8,128)} %bitcast.7, f32[40,1,640]{2,1,0:T(1,128)S(1)} %copy-done.1, s32[16,2]{1,0:T(8,128)S(1)} %copy.9.source_ref, s32[2]{0:T(128)S(1)} %copy-done.2, ...), custom_call_target="tpu_custom_call" | custom-call | tf_op jit(solution)/shard_map/pallas_call | solution.py:562
  112.7 0.7 copy.10
  113.5 0.7 copy.11
Async XLA Ops:
  1.4 0.9 copy-start
  2.3 0.9 copy-start.1
  3.2 0.7 copy-start.2
  3.8 0.7 copy-start.3

commit v6 on v5

--- a/solution.py
+++ b/solution.py
@@ -126,17 +126,24 @@
     return gain, sine, cosine, lam
 
 
+def row_chunks(rows):
+    groups = rows // ROWS
+    first = (groups + 1) // 2 * ROWS
+    spans = [(0, first)] + ([(first, rows - first)] if rows > first else [])
+    return len(spans), spans
+
+
 def kernel(
     dims, sec, psi_hbm, left_hbm, right_hbm, den_hbm, source_ref, owner_ref, orders_ref,
     new_ref, corr_ref, *scratch
 ):
     far, near, core = dims
-    chunks = psi_hbm.shape[0] // ROWS
+    chunks, spans = row_chunks(psi_hbm.shape[0])
     rows = psi_hbm.shape[0]
     width = psi_hbm.shape[2]
     op = far * near * core
     held = (scratch[:chunks], scratch[chunks : 2 * chunks])
-    (left_f, right_f, left_h, left_l, right_h, right_l, inner, vector_h, vector_l, inner_h, inner_l, raw,
+    (left_f, right_f, left_h, left_l, right_h, right_l, vector_h, vector_l, inner_h, inner_l, raw,
      applied, step, parts, got_core, got_near, got_far, picked, got_picked, chosen, psi_v, den_v, tiles, got_tiles, load_sem,
      gather_send, gather_recv, sum_send, sum_recv, tile_send, tile_recv) = scratch[2 * chunks :]
 
@@ -147,6 +154,9 @@
     a = lax.div(me, core * near)
     where = {"far": a, "near": b, "core": c, "sec": y}
     size = {"far": far, "near": near, "core": core, "sec": sec}
+
+    def at_rows(k):
+        return pl.ds(spans[k][0], spans[k][1])
 
     def turned(axis, by):
         place = dict(where)
@@ -196,7 +206,7 @@
     loads[2].wait()
     raw[...] = psi_v[...] * mask
     for k in range(chunks):
-        held[0][k][y, a, b] = raw[pl.ds(k * ROWS, ROWS), :]
+        held[0][k][y, a, b] = raw[at_rows(k), :]
 
     pl.semaphore_wait(barrier, len(around + along_far))
 
@@ -205,8 +215,6 @@
         return (pick("sec"), pick("far"), pick("near"))
 
     def sequence(k):
-        if k % 5 == 4:
-            return ("near", "sec", "far")
         return ("far", "near", "sec") if k % 2 == 0 else ("far", "sec", "near")
 
     slot_of = {pair: n for n, pair in enumerate(every)}
@@ -234,7 +242,8 @@
     def pick_copy(turn, k, d):
         n = slot_of[("core", d)]
         return pltpu.make_async_remote_copy(
-            src_ref=picked.at[turn, k, d - 1], dst_ref=got_picked.at[turn, k, d - 1],
+            src_ref=picked.at[turn, d - 1, :, :, at_rows(k)],
+            dst_ref=got_picked.at[turn, d - 1, :, :, at_rows(k)],
             send_sem=gather_send.at[turn, k, n], recv_sem=gather_recv.at[turn, k, n],
             device_id=device(turned("core", d)), device_id_type=MESH,
         )
@@ -242,14 +251,16 @@
     def pick_start(turn, k):
         for d in range(1, core):
             term = me - c + lax.rem(c + d, core)
-            picked[turn, k, d - 1] = held[turn][k][owner_ref[source_ref[term, sector]]]
+            picked[turn, d - 1, :, :, at_rows(k)] = held[turn][k][owner_ref[source_ref[term, sector]]]
             pick_copy(turn, k, d).start()
 
     def pick_wait(turn, k):
-        chosen[:, :, c] = held[turn][k][source]
+        chosen[:, :, c, at_rows(k)] = held[turn][k][source]
         for d in range(1, core):
             pick_copy(turn, k, d).wait_recv()
-            chosen[:, :, lax.rem(c + core - d, core)] = got_picked[turn, k, d - 1]
+            chosen[:, :, lax.rem(c + core - d, core), at_rows(k)] = got_picked[
+                turn, d - 1, :, :, at_rows(k)
+            ]
 
     def gather_end(turn):
         for k in range(chunks):
@@ -301,7 +312,8 @@
     def core_copy(turn, k, d):
         place = turned("core", d)
         return pltpu.make_async_remote_copy(
-            src_ref=parts.at[turn, k, :, :, place["core"]], dst_ref=got_core.at[turn, k, d - 1],
+            src_ref=parts.at[turn, :, :, place["core"], at_rows(k)],
+            dst_ref=got_core.at[turn, d - 1, :, :, at_rows(k)],
             send_sem=sum_send.at[turn, k, slot_of[("core", d)]],
             recv_sem=sum_recv.at[turn, k, slot_of[("core", d)]],
             device_id=device(place), device_id_type=MESH,
@@ -315,11 +327,11 @@
         place = turned(axis, d)
         if axis == "near":
             row = slice(None) if stage == 0 else a
-            source_ref, target_ref = parts.at[turn, k, row, place["near"], c], got_near
+            source_ref, target_ref = parts.at[turn, row, place["near"], c, at_rows(k)], got_near
         else:
             row = slice(None) if stage == 0 else b
-            source_ref, target_ref = parts.at[turn, k, place["far"], row, c], got_far
-        target = (turn, k, d - 1) if stage == 0 else (turn, k, d - 1, 0)
+            source_ref, target_ref = parts.at[turn, place["far"], row, c, at_rows(k)], got_far
+        target = (turn, d - 1, slice(None) if stage == 0 else 0, at_rows(k))
         return pltpu.make_async_remote_copy(
             src_ref=source_ref, dst_ref=target_ref.at[target],
             send_sem=sum_send.at[turn, k, slot_of[(axis, d)]],
@@ -330,10 +342,10 @@
     def sum_core(turn, k):
         for d in range(1, core):
             core_copy(turn, k, d).wait_recv()
-        mine = parts[turn, k, :, :, c]
+        mine = parts[turn, :, :, c, at_rows(k)]
         for d in range(1, core):
-            mine = mine + got_core[turn, k, d - 1]
-        parts[turn, k, :, :, c] = mine
+            mine = mine + got_core[turn, d - 1, :, :, at_rows(k)]
+        parts[turn, :, :, c, at_rows(k)] = mine
         for d in range(1, size[sum_axes(k)[0]]):
             sum_copy(turn, k, 0, d).start()
         return mine
@@ -341,11 +353,11 @@
     def sum_first(turn, k):
         first, second = sum_axes(k)
         got = got_near if first == "near" else got_far
-        index = (turn, k, slice(None), b, c) if first == "near" else (turn, k, a, slice(None), c)
+        index = (turn,) + ((slice(None), b) if first == "near" else (a, slice(None))) + (c, at_rows(k))
         mine = parts[index]
         for d in range(1, size[first]):
             sum_copy(turn, k, 0, d).wait_recv()
-            mine = mine + got[turn, k, d - 1]
+            mine = mine + got[turn, d - 1, :, at_rows(k)]
         parts[index] = mine
         for d in range(1, size[second]):
             sum_copy(turn, k, 1, d).start()
@@ -353,10 +365,10 @@
     def sum_second(turn, k):
         second = sum_axes(k)[1]
         got = got_near if second == "near" else got_far
-        mine = parts[turn, k, a, b, c]
+        mine = parts[turn, a, b, c, at_rows(k)]
         for d in range(1, size[second]):
             sum_copy(turn, k, 1, d).wait_recv()
-            mine = mine + got[turn, k, d - 1, 0]
+            mine = mine + got[turn, d - 1, 0, at_rows(k)]
         return mine
 
     def sum_end(turn):
@@ -386,27 +398,21 @@
                 pick_start(turn, k)
             if k > 0:
                 pick_wait(turn, k - 1)
-                high, low = split(chosen[...].reshape(op * ROWS, width))
-                vector_h[k - 1] = high
-                vector_l[k - 1] = low
-        full = (op * rows, width)
+        high, low = split(chosen[...].reshape(op * rows, width))
+        vector_h[...] = high
+        vector_l[...] = low
         for start, wide in tiles_n:
             cols = pl.ds(start, wide)
-            out = product3(
-                vector_h[...].reshape(full), vector_l[...].reshape(full),
-                right_h[:, cols], right_l[:, cols],
-            ).reshape(chunks, op, ROWS, wide)
-            for k in range(chunks):
-                inner[:, pl.ds(k * ROWS, ROWS), :wide] = out[k]
-            high, low = split(inner[:, :, :wide].reshape(op * rows, wide))
+            high, low = split(
+                product3(vector_h[...], vector_l[...], right_h[:, cols], right_l[:, cols])
+            )
             inner_h[:, cols] = high
             inner_l[:, cols] = low
         for start, wide in tiles_n:
             cols = pl.ds(start, wide)
-            parts[turn, :, :, :, :, :, cols] = product3(
-                left_h[...].reshape(full), left_l[...].reshape(full),
-                inner_h[:, cols], inner_l[:, cols],
-            ).reshape(chunks, far, near, core, ROWS, wide)
+            parts[turn, :, :, :, :, cols] = product3(
+                left_h[...], left_l[...], inner_h[:, cols], inner_l[:, cols]
+            ).reshape(far, near, core, rows, wide)
         for k in range(chunks):
             for d in range(1, core):
                 core_copy(turn, k, d).start()
@@ -438,9 +444,10 @@
     loads[3].wait()
 
     def split_left(k):
-        high, low = split(left_f[:, pl.ds(k * ROWS, ROWS), :].reshape(op * ROWS, width))
-        left_h[k] = high
-        left_l[k] = low
+        if k == 0:
+            high, low = split(left_f[...])
+            left_h[...] = high
+            left_l[...] = low
 
     gather_rest(0, split_left)
     start_part = matmuls(0, lambda k: held[0][k][y])
@@ -456,9 +463,9 @@
     def take_step(k, values):
         scale, rayleigh = values
         kept["scale"], kept["rayleigh"] = values
-        here = pl.ds(k * ROWS, ROWS)
+        here = at_rows(k)
         v_zero = scale * raw[here, :]
-        w_zero = scale * (sum_second(0, k) * mask[k * ROWS : (k + 1) * ROWS])
+        w_zero = scale * (sum_second(0, k) * mask[spans[k][0] : sum(spans[k])])
         update = (w_zero - rayleigh * v_zero) / den_v[here, :]
         applied[here, :] = w_zero
         step[here, :] = update
@@ -494,9 +501,9 @@
 
     def give(k, values):
         gain, sine, cosine, lam = values
-        here = pl.ds(k * ROWS, ROWS)
+        here = at_rows(k)
         w_zero = applied[here, :]
-        w_one = gain * (sum_second(1, k) * mask[k * ROWS : (k + 1) * ROWS] - along * w_zero)
+        w_one = gain * (sum_second(1, k) * mask[spans[k][0] : sum(spans[k])] - along * w_zero)
         new_vector = sine * (scale * raw[here, :]) - cosine * (gain * step[here, :])
         mixed = sine * w_zero - cosine * w_one
         new_ref[here, :] = new_vector
@@ -517,37 +524,26 @@
     rows, _, width = psi.shape
     far, near, core = dims
     op = far * near * core
-    chunks = rows // ROWS
+    chunks, spans = row_chunks(rows)
     peers = far + near + core + sec - 4
     pairs = near * core * sec - 1 + far - 1
     vmem = pl.BlockSpec(memory_space=pltpu.VMEM)
     smem = pl.BlockSpec(memory_space=pltpu.SMEM)
     hbm = pl.BlockSpec(memory_space=pl.ANY)
-    block = (ROWS, width)
-    scratch = [pltpu.VMEM((sec, far, near) + block, F32)] * (2 * chunks) + [
-        pltpu.VMEM((op, rows, width), F32),
-        pltpu.VMEM((width, width), F32),
-        pltpu.VMEM((chunks, op * ROWS, width), BF16),
-        pltpu.VMEM((chunks, op * ROWS, width), BF16),
-        pltpu.VMEM((width, width), BF16),
-        pltpu.VMEM((width, width), BF16),
-        pltpu.VMEM((op, rows, min(TILE, width)), F32),
-        pltpu.VMEM((chunks, op * ROWS, width), BF16),
-        pltpu.VMEM((chunks, op * ROWS, width), BF16),
-        pltpu.VMEM((op * rows, width), BF16),
-        pltpu.VMEM((op * rows, width), BF16),
-        pltpu.VMEM((rows, width), F32),
-        pltpu.VMEM((rows, width), F32),
-        pltpu.VMEM((rows, width), F32),
-        pltpu.VMEM((2, chunks, far, near, core) + block, F32),
-        pltpu.VMEM((2, chunks, core - 1, far, near) + block, F32),
-        pltpu.VMEM((2, chunks, near - 1, far) + block, F32),
-        pltpu.VMEM((2, chunks, far - 1, near) + block, F32),
-        pltpu.VMEM((2, chunks, core - 1, far, near) + block, F32),
-        pltpu.VMEM((2, chunks, core - 1, far, near) + block, F32),
+    block = (rows, width)
+    square = (width, width)
+    scratch = [pltpu.VMEM((sec, far, near, size, width), F32) for _, size in spans] * 2
+    scratch += [pltpu.VMEM(square, F32)] * 2 + [pltpu.VMEM(square, BF16)] * 8
+    scratch += [pltpu.VMEM(block, F32)] * 3 + [
+        pltpu.VMEM((2, far, near, core) + block, F32),
+        pltpu.VMEM((2, core - 1, far, near) + block, F32),
+        pltpu.VMEM((2, near - 1, far) + block, F32),
+        pltpu.VMEM((2, far - 1, near) + block, F32),
+        pltpu.VMEM((2, core - 1, far, near) + block, F32),
+        pltpu.VMEM((2, core - 1, far, near) + block, F32),
         pltpu.VMEM((far, near, core) + block, F32),
-        pltpu.VMEM((rows, width), F32),
-        pltpu.VMEM((rows, width), F32),
+        pltpu.VMEM(block, F32),
+        pltpu.VMEM(block, F32),
         pltpu.VMEM((3, 3, 8, 128), F32),
         pltpu.VMEM((3, pairs, 8, 128), F32),
         pltpu.SemaphoreType.DMA((4,)),
@@ -570,7 +566,7 @@
         ),
     )(
         psi,
-        left_env.reshape(op, rows, width),
+        left_env.reshape(width, width),
         right_env.reshape(width, width),
         denominators,
         source_sector,

time: 114 us -> 106 us (0.930)
  Pallas kernels: 108 us -> 99.8 us
    pallas_call x1, Pallas kernels: 108 us -> 99.8 us  [fused(): pl.pallas_call(functools.partial(kernel, dims, sec), out_shape=(flat, fla...]
where the time goes in v6:
time: 106 us
  Pallas kernels  99.8 us (94%)
  local copies, waits for them, and re-layouts  5.35 us (5%)
    pallas_call x1, Pallas kernels, fused(): pl.pallas_call(functools.partial(kernel, dims, sec), out_shape=(flat, fla...  99.8 us
    unnamed x11, local copies, waits for them, and re-layouts  5.35 us

profile of v6, /device:TPU:0, one launch (start us, length us, event | category | flops | bytes accessed | tf_op | source)
XLA Modules:
  0.0 105.7 jit_solution(14336795268807529266)
XLA Ops:
  0.6 0.8 copy.9.source_ref
  1.4 0.0 copy-start
  1.4 0.9 copy-done
  2.3 0.0 copy-start.1
  2.3 0.9 copy-done.1
  3.2 0.0 copy-start.2
  3.2 0.7 copy-done.2
  3.8 0.0 copy-start.3
  3.8 0.7 copy-done.3
  4.5 99.8 %shard_map.86 = (f32[40,640]{1,0:T(8,128)S(1)}, f32[40,640]{1,0:T(8,128)S(1)}) custom-call(f32[40,1,640]{2,1,0:T(1,128)S(1)} %copy-done, f32[640,640]{1,0:T(8,128)} %bitcast.6, f32[640,640]{1,0:T(8,128)} %bitcast.7, f32[40,1,640]{2,1,0:T(1,128)S(1)} %copy-done.1, s32[16,2]{1,0:T(8,128)S(1)} %copy.9.source_ref, s32[2]{0:T(128)S(1)} %copy-done.2, s32[2]{0:T(128)S(1)} %copy-done.3), custom_call_target="tpu_custom_call" | custom-call | tf_op jit(solution)/shard_map/pallas_call | solution.py:558
  104.2 0.7 copy.10
  105.0 0.7 copy.11
Async XLA Ops:
  1.4 0.9 copy-start
  2.3 0.9 copy-start.1
  3.2 0.7 copy-start.2
  3.8 0.7 copy-start.3
